TPU v7x, 256 devices: a whole 4x4x8 slice. The times are simulated.
256 devices in a mesh: row: 64 (over z, y, core), col: 4 (over x).
Axes of the slice: x: 4, y: 4, z: 8, core: 2. Of those that a mesh axis runs over, the one named last changes fastest.
Arguments:
- pair: bfloat16 [2048, 2048, 128], P(('row', 'col')), may hold values from -6 to 6
- pair_mask: int32 [2048, 2048], P(('row', 'col')), may hold values 0 or 1
- in_gain: float32 [128], replicated, may hold values from 0.25 to 1.75
- in_bias: float32 [128], replicated, may hold values from -3 to 3
- w_proj: bfloat16 [128, 512], replicated, may hold values from -0.5 to 0.5
- w_gate: bfloat16 [128, 128], replicated, may hold values from -0.5 to 0.5
- out_gain: float32 [128], replicated, may hold values from 0.25 to 1.75
- out_bias: float32 [128], replicated, may hold values from -3 to 3
- w_out: bfloat16 [128, 128], replicated, may hold values from -0.5 to 0.5
Outputs:
- update: bfloat16 [2048, 2048, 128], P(('row', 'col'))
All inputs are finite; a program needn't handle non-finite values. No bound on the sum of `pair_mask` on one device may be relied on, other than what follows from the above.
Results may differ from a plain program's by a relative error of at most 0.0056.
Values may be sent and summed in bfloat16 or wider, within the bound.
No kernel may reach another device: no remote copies, remote signals or barrier semaphores. Data moves between devices by JAX's collectives and lax.ppermute only.
A program may use at most 320 MiB of HBM per device.

v0:
```python
import jax
import jax.numpy as jnp
from jax import lax
from jax.sharding import PartitionSpec as P


def layer_norm(values, gain, bias):
    average = jnp.mean(values, axis=-1, keepdims=True)
    centred = values - average
    spread = jnp.mean(centred * centred, axis=-1, keepdims=True)
    return centred * lax.rsqrt(spread + 1e-05) * gain + bias


def shards(pair, pair_mask, in_gain, in_bias, w_proj, w_gate, out_gain, out_bias, w_out):
    row_count, total, channels = pair.shape
    hidden_units = w_out.shape[0]
    n_row = lax.axis_size("row")
    n_col = lax.axis_size("col")
    normed = layer_norm(pair.astype(jnp.float32), in_gain, in_bias).astype(jnp.bfloat16)
    keep_mask = pair_mask.astype(jnp.float32)[None]

    def project(offset):
        return jnp.einsum(
            "ikc,ch->hik",
            normed,
            w_proj[:, offset : offset + hidden_units],
            preferred_element_type=jnp.float32,
        )

    left_part = (keep_mask * jax.nn.sigmoid(project(0)) * project(hidden_units)).astype(
        jnp.bfloat16
    )
    right_part = (
        keep_mask * jax.nn.sigmoid(project(2 * hidden_units)) * project(3 * hidden_units)
    ).astype(jnp.bfloat16)
    left_shard, right_shard = (
        lax.all_to_all(left_part, "row", split_axis=0, concat_axis=1, tiled=True),
        lax.all_to_all(right_part, "row", split_axis=0, concat_axis=1, tiled=True),
    )
    group_rows = left_shard.shape[1]
    own_channels = left_shard.shape[0]
    product = jnp.einsum(
        "hik,hjk->hij",
        lax.all_gather(left_shard, "col", axis=1, tiled=True),
        right_shard,
        preferred_element_type=jnp.float32,
    ).astype(jnp.bfloat16)
    product = product.reshape(own_channels, n_col, group_rows, group_rows)
    returned = lax.all_to_all(
        lax.all_to_all(product, "row", split_axis=2, concat_axis=0, tiled=True),
        "col",
        split_axis=1,
        concat_axis=3,
        tiled=True,
    )
    values = returned.reshape(hidden_units, row_count, n_col, n_row, row_count).astype(jnp.float32)
    average = jnp.mean(values, axis=0, keepdims=True)
    centred = values - average
    spread = jnp.mean(centred * centred, axis=0, keepdims=True)
    post_norm = (
        centred * lax.rsqrt(spread + 1e-05) * out_gain.reshape(-1, 1, 1, 1, 1)
        + out_bias.reshape(-1, 1, 1, 1, 1)
    ).astype(jnp.bfloat16)
    projected = jnp.einsum("hiabt,hc->ibatc", post_norm, w_out, preferred_element_type=jnp.float32)
    projected = projected.reshape(row_count, total, channels)
    gate_value = jax.nn.sigmoid(
        jnp.einsum("ijc,cd->ijd", normed, w_gate, preferred_element_type=jnp.float32)
    )
    return (gate_value * projected).astype(jnp.bfloat16)


def solution(mesh):
    return jax.shard_map(
        shards,
        mesh=mesh,
        in_specs=(
            P(("row", "col"), None, None),
            P(("row", "col"), None),
            P(),
            P(),
            P(),
            P(),
            P(),
            P(),
            P(),
        ),
        out_specs=P(("row", "col"), None, None),
        check_vma=False,
    )
```

profile of v0, /device:TPU:6, one launch (start us, length us, event | category | flops | bytes accessed | tf_op | source)
XLA Modules:
  0.0 527.0 jit_solution(16843505803495760037)
XLA Ops:
  6.5 0.0 copy-start
  6.5 0.0 copy-start.8
  6.5 0.0 copy-start.9
  6.5 0.0 copy-start.4
  6.5 0.0 all-gather.2.cloned.1.call-start
  6.6 0.0 copy-start.1
  6.6 1.0 convert_element_type.44
  7.6 3.7 convert_reduce_fusion
  11.3 6.0 %fusion.4 = f32[8,2048]{1,0:T(8,128)S(1)} fusion(bf16[8,2048,128]{2,1,0:T(8,128)(2,1)} %param.9, f32[8,2048]{1,0:T(8,128)S(1)} %broadcast_multiply_fusion), kind=kLoop, calls=%fused_computation.8 | loop fusion | flops 8372224 | bytes 4325376 | tf_op jit(solution)/shard_map/reduce_sum | solution.py:10
  17.3 0.0 copy-done.8
  17.3 0.0 copy-done.9
  17.4 0.0 copy-done.4
  17.4 0.0 copy-done.1
  17.4 4.5 fusion.40
  21.9 8.7 %fusion.29 = bf16[128,8,2048]{0,2,1:T(8,128)(2,1)} fusion(f32[8,2048,128]{2,1,0:T(8,128)S(1)} %fusion.40, f32[8,2048]{1,0:T(8,128)S(1)} %convert_element_type.44, bf16[128,512]{1,0:T(8,128)(2,1)S(1)} %copy-done.4, bf16[8,2048,128]{2,1,0:T(8,128)(2,1)S(1)} %copy-done.1, f32[128]{0:T(128)S(1)} %copy-done.8, f32[128]{0:T(128)S(1)} %copy-done.9, ...), kind=kOutput, calls=%fused_computation.35 | convolution fusion | flops 562036736 | bytes 17007616 | tf_op jit(solution)/shard_map/ikc,ch->hik/dot_general | solution.py:23
  30.6 6.7 %copy.58 = bf16[128,8,2048]{2,1,0:T(8,128)(2,1)} copy(bf16[128,8,2048]{0,2,1:T(8,128)(2,1)} %fusion.29) | data formatting | bytes 8388608 | tf_op jit(solution)/shard_map/convert_element_type | solution.py:30
  37.3 108.4 %all_to_all.63 = bf16[128,8,2048]{2,1,0:T(8,128)(2,1)S(1)} all-to-all(bf16[128,8,2048]{2,1,0:T(8,128)(2,1)} %copy.58), channel_id=1, replica_groups=mesh['row'=64,'col'=4] {'row'}, dimensions={0} | all-to-all | bytes 8388608 | tf_op jit(solution)/shard_map/all_to_all | solution.py:37
  145.7 2.3 copy.95
  148.0 0.0 all-gather.2.cloned.1.call-update
  148.1 0.0 copy-start.2
  148.1 8.1 %fusion.37 = f32[8,2048,128]{2,1,0:T(8,128)S(1)} fusion(bf16[128,512]{1,0:T(8,128)(2,1)S(1)} %copy-done.4, bf16[8,2048,128]{2,1,0:T(8,128)(2,1)} %param.9, f32[128]{0:T(128)S(1)} %copy-done.8, f32[128]{0:T(128)S(1)} %copy-done.9, f32[8,2048]{1,0:T(8,128)S(1)} %add_rsqrt_fusion, f32[8,2048]{1,0:T(8,128)S(1)} %broadcast_multiply_fusion), kind=kOutput, calls=%fused_computation.44 | convolution fusion | flops 549453824 | bytes 12747776 | tf_op jit(solution)/shard_map/ikc,ch->hik/dot_general | solution.py:23
  156.2 0.0 copy-done.2
  156.2 8.7 %fusion.30 = bf16[128,8,2048]{0,2,1:T(8,128)(2,1)} fusion(f32[8,2048,128]{2,1,0:T(8,128)S(1)} %fusion.37, f32[8,2048]{1,0:T(8,128)S(1)} %convert_element_type.44, bf16[128,512]{1,0:T(8,128)(2,1)S(1)} %copy-done.4, bf16[8,2048,128]{2,1,0:T(8,128)(2,1)S(1)} %copy-done.2, f32[128]{0:T(128)S(1)} %copy-done.8, f32[128]{0:T(128)S(1)} %copy-done.9, ...), kind=kOutput, calls=%fused_computation.36 | convolution fusion | flops 562036736 | bytes 17007616 | tf_op jit(solution)/shard_map/ikc,ch->hik/dot_general | solution.py:23
  164.9 6.9 %copy.60 = bf16[128,8,2048]{2,1,0:T(8,128)(2,1)} copy(bf16[128,8,2048]{0,2,1:T(8,128)(2,1)} %fusion.30) | data formatting | bytes 8388608 | tf_op jit(solution)/shard_map/convert_element_type | solution.py:35
  171.8 101.9 %all_to_all.64 = bf16[128,8,2048]{2,1,0:T(8,128)(2,1)} all-to-all(bf16[128,8,2048]{2,1,0:T(8,128)(2,1)} %copy.60), channel_id=1, replica_groups=mesh['row'=64,'col'=4] {'row'}, dimensions={0} | all-to-all | bytes 8388608 | tf_op jit(solution)/shard_map/all_to_all | solution.py:38
  273.7 26.1 %all-gather.2.cloned.1.call-done = bf16[2,2048,2048]{2,1,0:T(8,128)(2,1)} async-done(((bf16[2,512,2048]{2,1,0:T(8,128)(2,1)}), bf16[2,2048,2048]{2,1,0:T(8,128)(2,1)}) %all-gather.2.cloned.1.call-update) | async-done | bytes 16777232 | tf_op jit(solution)/shard_map/all_gather | solution.py:44
  299.8 13.7 %fusion.26 = bf16[2,2048,512]{2,1,0:T(8,128)(2,1)S(1)} fusion(bf16[2,2048,2048]{2,1,0:T(8,128)(2,1)} %all-gather.2.cloned.1.call-done, bf16[2,64,8,2048]{3,2,0,1:T(8,128)(2,1)} %bitcast.96), kind=kOutput, calls=%fused_computation.34 | convolution fusion | flops 8592031744 | bytes 25165824 | tf_op jit(solution)/shard_map/hik,hjk->hij/dot_general | solution.py:42
  313.5 3.2 copy.62
  316.7 106.8 %all_to_all.65 = bf16[2,4,512,512]{3,1,0,2:T(4,128)(2,1)S(1)} all-to-all(bf16[2,4,512,512]{3,1,0,2:T(4,128)(2,1)S(1)} %copy.62), channel_id=1, replica_groups=mesh['row'=64,'col'=4] {'row'}, dimensions={2} | all-to-all | bytes 8388608 | tf_op jit(solution)/shard_map/all_to_all | solution.py:50
  423.6 1.4 copy.94
  425.0 0.6 copy.64
  425.6 0.4 copy.65
  426.0 50.6 %all_to_all.66 = bf16[128,4,8,512]{3,2,0,1:T(8,128)(2,1)} all-to-all(bf16[128,4,8,512]{3,2,0,1:T(8,128)(2,1)S(1)} %copy.65), channel_id=1, replica_groups=mesh['row'=64,'col'=4] {'col'}, dimensions={1} | all-to-all | bytes 8388608 | tf_op jit(solution)/shard_map/all_to_all | solution.py:49
  476.6 0.0 copy-start.6
  476.6 0.0 copy-start.7
  476.6 7.9 %copy.66 = bf16[128,4,8,512]{0,3,1,2:T(8,128)(2,1)} copy(bf16[128,4,8,512]{3,2,0,1:T(8,128)(2,1)} %all_to_all.66) | data formatting | bytes 8388608 | tf_op jit(solution)/shard_map/all_to_all | solution.py:49
  484.5 3.4 fusion
  488.0 0.6 div.37
  488.6 6.0 %fusion.9 = f32[8,4,512]{2,1,0:T(4,128)S(1)} fusion(bf16[128,4,8,512]{0,3,1,2:T(8,128)(2,1)} %copy.66, f32[8,4,512]{2,1,0:T(4,128)S(1)} %copy.69), kind=kLoop, calls=%fused_computation.13 | loop fusion | flops 8372224 | bytes 4325376 | tf_op jit(solution)/shard_map/reduce_sum | solution.py:59
  494.6 0.6 rsqrt.21
  495.2 0.0 copy-done
  495.2 0.0 copy-done.6
  495.2 0.0 copy-done.7
  495.2 6.7 %fusion.31 = f32[8,64,4,8,128]{4,3,1,2,0:T(8,128)S(1)} fusion(bf16[128,4,8,512]{0,3,1,2:T(8,128)(2,1)} %copy.66, f32[128]{0:T(128)S(1)} %copy-done.6, f32[128]{0:T(128)S(1)} %copy-done.7, bf16[128,128]{1,0:T(8,128)(2,1)S(1)} %copy-done, f32[8,4,64,8]{3,2,0,1:T(8,128)S(1)} %rsqrt.21, f32[8,4,64,8]{3,2,0,1:T(8,128)S(1)} %div.37), kind=kOutput, calls=%fused_computation.37 | convolution fusion | flops 549453824 | bytes 12747776 | tf_op jit(solution)/shard_map/hiabt,hc->ibatc/dot_general | solution.py:64
  501.9 0.0 copy-start.3
  501.9 0.0 copy-start.5
  502.0 4.4 copy.72
  506.3 0.0 copy-done.3
  506.3 0.0 copy-done.5
  506.3 13.8 %fusion.15 = bf16[8,2048,128]{2,1,0:T(8,128)(2,1)} fusion(f32[8,64,4,8,128]{4,3,2,1,0:T(8,128)} %copy.72, bf16[128,128]{1,0:T(8,128)(2,1)S(1)} %copy-done.5, bf16[8,2048,128]{2,1,0:T(8,128)(2,1)S(1)} %copy-done.3, f32[128]{0:T(128)S(1)} %copy-done.8, f32[128]{0:T(128)S(1)} %copy-done.9, f32[8,2048]{1,0:T(8,128)S(1)} %add_rsqrt_fusion, ...), kind=kOutput, calls=%fused_computation.20 | convolution fusion | flops 559939584 | bytes 16942080 | tf_op jit(solution)/shard_map/ijc,cd->ijd/dot_general | solution.py:67
  (5 shorter events, 0.1 us)
Async XLA Ops:
  6.5 488.7 %copy-start = (bf16[128,128]{1,0:T(8,128)(2,1)S(1)}, bf16[128,128]{1,0:T(8,128)(2,1)}, u32[]{:S(2)}) copy-start(bf16[128,128]{1,0:T(8,128)(2,1)} %param.17) | copy-start | bytes 98308
  6.5 10.8 %copy-start.8 = (f32[128]{0:T(128)S(1)}, f32[128]{0:T(128)}, u32[]{:S(2)}) copy-start(f32[128]{0:T(128)} %param.12) | copy-start | bytes 1540
  6.5 10.8 %copy-start.9 = (f32[128]{0:T(128)S(1)}, f32[128]{0:T(128)}, u32[]{:S(2)}) copy-start(f32[128]{0:T(128)} %param.11) | copy-start | bytes 1540
  6.5 10.8 %copy-start.4 = (bf16[128,512]{1,0:T(8,128)(2,1)S(1)}, bf16[128,512]{1,0:T(8,128)(2,1)}, u32[]{:S(2)}) copy-start(bf16[128,512]{1,0:T(8,128)(2,1)} %param.13) | copy-start | bytes 393220
  6.5 293.3 %all-gather.2.cloned.1.call-start = ((), (), s32[]{:S(2)}) async-start(), calls=%async_computation.4 | async-start | bytes 20971520 | tf_op jit(solution)/shard_map/all_gather | solution.py:44
  6.6 10.8 %copy-start.1 = (bf16[8,2048,128]{2,1,0:T(8,128)(2,1)S(1)}, bf16[8,2048,128]{2,1,0:T(8,128)(2,1)}, u32[]{:S(2)}) copy-start(bf16[8,2048,128]{2,1,0:T(8,128)(2,1)} %param.9) | copy-start | bytes 12582916
  148.1 8.1 %copy-start.2 = (bf16[8,2048,128]{2,1,0:T(8,128)(2,1)S(1)}, bf16[8,2048,128]{2,1,0:T(8,128)(2,1)}, u32[]{:S(2)}) copy-start(bf16[8,2048,128]{2,1,0:T(8,128)(2,1)} %param.9) | copy-start | bytes 12582916
  476.6 18.6 %copy-start.6 = (f32[128]{0:T(128)S(1)}, f32[128]{0:T(128)}, u32[]{:S(2)}) copy-start(f32[128]{0:T(128)} %param.16) | copy-start | bytes 1540
  476.6 18.6 %copy-start.7 = (f32[128]{0:T(128)S(1)}, f32[128]{0:T(128)}, u32[]{:S(2)}) copy-start(f32[128]{0:T(128)} %param.15) | copy-start | bytes 1540
  501.9 4.4 copy-start.3
  501.9 4.4 copy-start.5
Sparse Core Ops, SparseCore 0:
  148.2 151.5 all-gather.1
where the time goes:
time: 530 us; the launch traced here: 527 us
  blocking collectives  368 us (69%)
  matrix products  64.2 us (12%)
  local copies, waits for them, and re-layouts  35.1 us (7%)
  waiting for transfers between devices  26.1 us (5%)
  other arithmetic  20.2 us (4%)
  between operations  13.6 us (3%)
    all_to_all x1, blocking collectives, shards(): lax.all_to_all(left_part, 'row', split_axis=0, concat_axis=1, tiled=True)  108 us
    all_to_all x1, blocking collectives, shards(): lax.all_to_all(product, 'row', split_axis=2, concat_axis=0, tiled=True)  107 us
    all_to_all x1, blocking collectives, shards(): lax.all_to_all(right_part, 'row', split_axis=0, concat_axis=1, tiled=True)  102 us
    all_to_all x1, blocking collectives, shards(): lax.all_to_all(lax.all_to_all(product, 'row', split_axis=2, concat_axis=0...  50.6 us
    dot_general x4, matrix products, project(): jnp.einsum('ikc,ch->hik', normed, w_proj[:, offset:offset + hidden_units]...  30.1 us
    all_gather x1, waiting for transfers between devices, shards(): lax.all_gather(left_shard, 'col', axis=1, tiled=True)  26.1 us
    dot_general x1, matrix products, shards(): jnp.einsum('ijc,cd->ijd', normed, w_gate, preferred_element_type=jnp.floa...  13.8 us
    dot_general x1, matrix products, shards(): jnp.einsum('hik,hjk->hij', lax.all_gather(left_shard, 'col', axis=1, tile...  13.7 us
  transfers between devices with their start and end apart: 1, of which 1 were waited for; matrix products, arithmetic and copies ran while one was open for 5% of the time, Pallas kernels for 0%

commit v1 on v0

v1 whole, which is shorter than its diff:
```python
import functools

import jax
import jax.numpy as jnp
from jax import lax
from jax.experimental import pallas as pl
from jax.experimental.pallas import tpu as pltpu
from jax.sharding import Mesh
from jax.sharding import PartitionSpec as P

NZ, NY, NCORE, NX = 8, 4, 2, 4
CHIPS = ("z", "y", "x")
ROWS = 8
LANES = 128
VMEM_LIMIT = 56 * 1024 * 1024


def rows_norm(x, gain, bias):
    average = jnp.mean(x, axis=-1, keepdims=True)
    centred = x - average
    spread = jnp.mean(centred * centred, axis=-1, keepdims=True)
    return centred * lax.rsqrt(spread + 1e-05) * gain + bias


def sigmoid(x):
    return 0.5 * jnp.tanh(0.5 * x) + 0.5


def enter_kernel(pair_ref, mask_ref, gain_ref, bias_ref, w_ref, left_ref, right_ref, normed_ref, lscr, rscr):
    hidden = w_ref.shape[0] // 4
    width = pair_ref.shape[1]
    gain = gain_ref[...]
    bias = bias_ref[...]
    keep = mask_ref[...].astype(jnp.float32)
    for i in range(ROWS):
        x = pair_ref[i].astype(jnp.float32)
        normed = rows_norm(x, gain, bias).astype(jnp.bfloat16)
        normed_ref[i] = normed
        for side, scr in ((0, lscr), (1, rscr)):
            proj = lax.dot_general(
                w_ref[2 * side * hidden : (2 * side + 2) * hidden],
                normed,
                (((1,), (1,)), ((), ())),
                preferred_element_type=jnp.float32,
            )
            value = sigmoid(proj[:hidden]) * proj[hidden:] * keep[i : i + 1]
            for t in range(width // LANES):
                scr[t, pl.ds(i, hidden, stride=ROWS), :] = value[:, t * LANES : (t + 1) * LANES]
    for t in range(width // LANES):
        lanes = pl.ds(t * LANES, LANES)
        left_ref[:, :, lanes] = lscr[t].reshape(hidden, ROWS, LANES).astype(jnp.bfloat16)
        right_ref[:, :, lanes] = rscr[t].reshape(hidden, ROWS, LANES).astype(jnp.bfloat16)


def enter(pair, mask, gain, bias, w_proj_t, width=256):
    rows, total, channels = pair.shape
    hidden = w_proj_t.shape[0] // 4
    whole = lambda *shape: pl.BlockSpec(shape, lambda k: (0,) * len(shape))
    side = jax.ShapeDtypeStruct((hidden, rows, total), jnp.bfloat16)
    side_spec = pl.BlockSpec((hidden, rows, width), lambda k: (0, 0, k))
    pair_spec = pl.BlockSpec((rows, width, channels), lambda k: (0, k, 0))
    return pl.pallas_call(
        enter_kernel,
        grid=(total // width,),
        in_specs=[
            pair_spec,
            pl.BlockSpec((rows, width), lambda k: (0, k)),
            whole(1, channels),
            whole(1, channels),
            whole(4 * hidden, channels),
        ],
        out_specs=[side_spec, side_spec, pair_spec],
        out_shape=[side, side, jax.ShapeDtypeStruct(pair.shape, jnp.bfloat16)],
        scratch_shapes=[pltpu.VMEM((width // LANES, hidden * rows, LANES), jnp.float32)] * 2,
        compiler_params=pltpu.CompilerParams(vmem_limit_bytes=VMEM_LIMIT),
        name="enter",
    )(pair, mask, gain, bias, w_proj_t)


def product_kernel(core_ref, a_ref, own_ref, other_ref, out_ref, b_scr, sems):
    @pl.when(pl.program_id(0) == 0)
    def _():
        core = core_ref[0]
        one = pltpu.make_async_copy(own_ref, b_scr.at[:, core], sems.at[0])
        two = pltpu.make_async_copy(other_ref, b_scr.at[:, 1 - core], sems.at[1])
        one.start()
        two.start()
        one.wait()
        two.wait()

    depth = a_ref.shape[1]
    out_ref[...] = lax.dot_general(
        a_ref[...],
        b_scr[...].reshape(-1, depth),
        (((1,), (1,)), ((), ())),
        preferred_element_type=jnp.float32,
    ).astype(jnp.bfloat16)


def product(core, a, own, other, height=128):
    m, depth = a.shape
    groups, part, _ = own.shape
    n = 2 * groups * part
    return pl.pallas_call(
        product_kernel,
        grid_spec=pltpu.PrefetchScalarGridSpec(
            num_scalar_prefetch=1,
            grid=(m // height,),
            in_specs=[
                pl.BlockSpec((height, depth), lambda i, c: (i, 0)),
                pl.BlockSpec(memory_space=pl.ANY),
                pl.BlockSpec(memory_space=pl.ANY),
            ],
            out_specs=pl.BlockSpec((height, n), lambda i, c: (i, 0)),
            scratch_shapes=[
                pltpu.VMEM((groups, 2, part, depth), jnp.bfloat16),
                pltpu.SemaphoreType.DMA((2,)),
            ],
        ),
        out_shape=jax.ShapeDtypeStruct((m, n), jnp.bfloat16),
        compiler_params=pltpu.CompilerParams(vmem_limit_bytes=VMEM_LIMIT),
        name="product",
    )(core, a, own, other)


def leave_kernel(prod_ref, normed_ref, gain_ref, bias_ref, w_out_ref, w_gate_ref, out_ref, scr):
    hidden, rows, width = prod_ref.shape
    values = prod_ref[...].astype(jnp.float32)
    average = jnp.sum(values, axis=0, keepdims=True) * (1.0 / hidden)
    centred = values - average
    spread = jnp.sum(centred * centred, axis=0, keepdims=True) * (1.0 / hidden)
    scaled = centred * lax.rsqrt(spread + 1e-05)
    for t in range(width // LANES):
        scr[t] = scaled[:, :, t * LANES : (t + 1) * LANES].reshape(hidden * rows, LANES)
    gain = gain_ref[...]
    bias = bias_ref[...]
    for i in range(rows):
        values = [scr[t, pl.ds(i, hidden, stride=rows), :] for t in range(width // LANES)]
        post = (jnp.concatenate(values, axis=1) * gain + bias).astype(jnp.bfloat16)
        projected = lax.dot_general(
            post, w_out_ref[...], (((0,), (0,)), ((), ())), preferred_element_type=jnp.float32
        )
        gate = jnp.dot(normed_ref[i], w_gate_ref[...], preferred_element_type=jnp.float32)
        out_ref[i] = (sigmoid(gate) * projected).astype(jnp.bfloat16)


def leave(prod, normed, gain, bias, w_out, w_gate, width=256):
    hidden, rows, total = prod.shape
    channels = normed.shape[2]
    whole = lambda *shape: pl.BlockSpec(shape, lambda k: (0,) * len(shape))
    pair_spec = pl.BlockSpec((rows, width, channels), lambda k: (0, k, 0))
    return pl.pallas_call(
        leave_kernel,
        grid=(total // width,),
        in_specs=[
            pl.BlockSpec((hidden, rows, width), lambda k: (0, 0, k)),
            pair_spec,
            whole(hidden, 1),
            whole(hidden, 1),
            whole(hidden, channels),
            whole(channels, channels),
        ],
        out_specs=pair_spec,
        out_shape=jax.ShapeDtypeStruct(normed.shape, jnp.bfloat16),
        scratch_shapes=[pltpu.VMEM((width // LANES, hidden * rows, LANES), jnp.float32)],
        compiler_params=pltpu.CompilerParams(vmem_limit_bytes=VMEM_LIMIT),
        name="leave",
    )(prod, normed, gain, bias, w_out, w_gate)


def shards(pair, pair_mask, in_gain, in_bias, w_proj, w_gate, out_gain, out_bias, w_out):
    rows, total, channels = pair.shape
    hidden = w_out.shape[0]
    left, right, normed = enter(
        pair, pair_mask, in_gain.reshape(1, -1), in_bias.reshape(1, -1), w_proj.T
    )
    exchange = functools.partial(lax.all_to_all, axis_name=CHIPS, split_axis=0, concat_axis=0, tiled=True)
    own = exchange(right)
    other = lax.ppermute(own, "core", [(0, 1), (1, 0)])
    a = exchange(left)
    groups = (NZ * NY, NX * rows, total)
    prod = product(
        lax.axis_index("core").reshape(1),
        a.reshape(hidden * rows, total),
        own.reshape(groups),
        other.reshape(groups),
    )
    back = exchange(prod.reshape(hidden, rows, total))
    return leave(
        back, normed, out_gain.reshape(-1, 1), out_bias.reshape(-1, 1), w_out, w_gate
    )


def solution(mesh):
    fine = Mesh(mesh.devices.reshape(NZ, NY, NCORE, NX), ("z", "y", "core", "x"))
    split = ("z", "y", "core", "x")
    return jax.shard_map(
        shards,
        mesh=fine,
        in_specs=(P(split), P(split), P(), P(), P(), P(), P(), P(), P()),
        out_specs=P(split),
        check_vma=False,
    )
```

time: 530 us -> 379 us (0.72)
  blocking collectives: 368 us -> 111 us
  waiting for transfers between devices: 26.1 us -> 189 us
  matrix products: 64.2 us -> 0 us
  Pallas kernels: 0 us -> 56.5 us
  local copies, waits for them, and re-layouts: 35.1 us -> 3.12 us
  other arithmetic: 20.2 us -> 0 us
  starting transfers between devices: 0.03 us -> 18.7 us
  between operations: 13.6 us -> 0.07 us
    all_to_all x4 -> x1, blocking collectives: 368 us -> 111 us  [shards(): own = exchange(right)]
    all_to_all x0 -> x2, waiting for transfers between devices: none -> 189 us  [the longest x1 95.2 us: shards(): a = exchange(left)]
    dot_general x7 -> x0, matrix products: 64.2 us -> none  [the longest x4 30.1 us: project(): jnp.einsum('ikc,ch->hik', normed, w_proj[:, offset:offset + hidden_units]...]
    pallas_call x0 -> x3, Pallas kernels: none -> 56.5 us  [the longest x1 28.3 us: product(): pl.pallas_call(product_kernel, grid_spec=pltpu.PrefetchScalarGridSpec(num...]
    all_gather x1 -> x0, waiting for transfers between devices: 26.1 us -> none  [shards(): lax.all_gather(left_shard, 'col', axis=1, tiled=True)]
    reduce_sum x4 -> x0, other arithmetic: 19.1 us -> none  [the longest x1 6 us: layer_norm(): spread = jnp.mean(centred * centred, axis=-1, keepdims=True)]
    all_to_all x0 -> x2, starting transfers between devices: none -> 18.6 us  [the longest x1 9.31 us: shards(): a = exchange(left)]
    convert_element_type x2 -> x0, local copies, waits for them, and re-layouts: 13.6 us -> none  [the longest x1 6.9 us: shards(): right_part = (keep_mask * jax.nn.sigmoid(project(2 * hidden_units)) * pro...]
  transfers between devices with their start and end apart: 1 -> 3, of which waited for: 1 -> 2; matrix products, arithmetic and copies ran while one was open for 5% -> 0% of each run, Pallas kernels for 0% -> 0%
where the time goes in v1:
time: 379 us
  waiting for transfers between devices  189 us (50%)
  blocking collectives  111 us (29%)
  Pallas kernels  56.5 us (15%)
  starting transfers between devices  18.7 us (5%)
    all_to_all x1, blocking collectives, shards(): own = exchange(right)  111 us
    all_to_all x1, waiting for transfers between devices, shards(): a = exchange(left)  95.2 us
    all_to_all x1, waiting for transfers between devices, shards(): back = exchange(prod.reshape(hidden, rows, total))  93.8 us
    pallas_call x1, Pallas kernels, product(): pl.pallas_call(product_kernel, grid_spec=pltpu.PrefetchScalarGridSpec(num...  28.3 us
    pallas_call x1, Pallas kernels, enter(): pl.pallas_call(enter_kernel, grid=(total // width,), in_specs=[pair_spec,...  17 us
    pallas_call x1, Pallas kernels, leave(): pl.pallas_call(leave_kernel, grid=(total // width,), in_specs=[pl.BlockSp...  11.2 us
    all_to_all x1, starting transfers between devices, shards(): a = exchange(left)  9.31 us
    all_to_all x1, starting transfers between devices, shards(): back = exchange(prod.reshape(hidden, rows, total))  9.28 us
  transfers between devices with their start and end apart: 3, of which 2 were waited for; matrix products, arithmetic and copies ran while one was open for 0% of the time, Pallas kernels for 0%

profile of v1, /device:TPU:6, one launch (start us, length us, event | category | flops | bytes accessed | tf_op | source)
XLA Modules:
  0.0 378.8 jit_solution(11704069080100174187)
XLA Ops:
  0.0 1.6 copy.10
  1.6 17.0 %enter.1 = (bf16[128,8,2048]{2,1,0:T(8,128)(2,1)}, bf16[128,8,2048]{2,1,0:T(8,128)(2,1)}, bf16[8,2048,128]{2,1,0:T(8,128)(2,1)}) custom-call(bf16[8,2048,128]{2,1,0:T(8,128)(2,1)} %pair_ref.1, s32[8,2048]{1,0:T(8,128)} %mask_ref.1, f32[1,128]{1,0:T(1,128)} %bitcast.13, f32[1,128]{1,0:T(1,128)} %bitcast.14, bf16[512,128]{1,0:T(8,128)(2,1)} %bitcast.12), custom_call_target="tpu_custom_call" | custom-call | tf_op jit(solution)/shard_map/enter/pallas_call | solution.py:62
  18.6 111.3 %all_to_all.15 = bf16[128,8,2048]{2,1,0:T(8,128)(2,1)} all-to-all(bf16[128,8,2048]{2,1,0:T(8,128)(2,1)} %get-tuple-element.9), channel_id=1, replica_groups=mesh['z'=8,'y'=4,'core'=2,'x'=4] {'z','y','x'}, dimensions={0} | all-to-all | bytes 8388608 | tf_op jit(solution)/shard_map/all_to_all | solution.py:178
  130.0 9.3 %all-to-all-start = ((bf16[128,8,2048]{2,1,0:T(8,128)(2,1)}), bf16[128,8,2048]{2,1,0:T(8,128)(2,1)}, u32[]{:S(2)}, u32[]{:S(2)}) async-start(bf16[128,8,2048]{2,1,0:T(8,128)(2,1)} %get-tuple-element.8), calls=%async_computation | async-start | bytes 8388608 | tf_op jit(solution)/shard_map/all_to_all | solution.py:180
  139.3 0.1 collective-permute-start
  139.4 95.2 %all-to-all-done = bf16[128,8,2048]{2,1,0:T(8,128)(2,1)} async-done(((bf16[128,8,2048]{2,1,0:T(8,128)(2,1)}), bf16[128,8,2048]{2,1,0:T(8,128)(2,1)}, u32[]{:S(2)}, u32[]{:S(2)}) %all-to-all-start) | async-done | bytes 4194336 | tf_op jit(solution)/shard_map/all_to_all | solution.py:180
  234.6 0.0 collective-permute-done
  234.6 28.3 %product.1 = bf16[1024,2048]{1,0:T(8,128)(2,1)} custom-call(s32[1]{0:T(128)} %bitcast.core_ref, bf16[1024,2048]{1,0:T(8,128)(2,1)} %bitcast.4.a_ref, bf16[32,32,2048]{2,1,0:T(8,128)(2,1)} %bitcast.10, bf16[32,32,2048]{2,1,0:T(8,128)(2,1)} %bitcast.6.other_ref), custom_call_target="tpu_custom_call" | custom-call | tf_op jit(solution)/shard_map/product/pallas_call | solution.py:104
  262.9 0.0 copy-start
  262.9 0.0 copy-start.1
  262.9 9.3 %all-to-all-start.2 = ((bf16[128,8,2048]{2,1,0:T(8,128)(2,1)}), bf16[128,8,2048]{2,1,0:T(8,128)(2,1)}, u32[]{:S(2)}, u32[]{:S(2)}) async-start(bf16[128,8,2048]{2,1,0:T(8,128)(2,1)} %bitcast.11), calls=%async_computation.2 | async-start | bytes 8388608 | tf_op jit(solution)/shard_map/all_to_all | solution.py:188
  272.2 0.0 copy-done
  272.2 0.7 copy.11.gain_ref
  273.0 0.0 copy-done.1
  273.0 0.7 copy.12.bias_ref
  273.7 93.8 %all-to-all-done.2.prod_ref = bf16[128,8,2048]{2,1,0:T(8,128)(2,1)} async-done(((bf16[128,8,2048]{2,1,0:T(8,128)(2,1)}), bf16[128,8,2048]{2,1,0:T(8,128)(2,1)}, u32[]{:S(2)}, u32[]{:S(2)}) %all-to-all-start.2) | async-done | bytes 4194336 | tf_op jit(solution)/shard_map/all_to_all | solution.py:188
  367.5 11.2 %leave.1 = bf16[8,2048,128]{2,1,0:T(8,128)(2,1)} custom-call(bf16[128,8,2048]{2,1,0:T(8,128)(2,1)} %all-to-all-done.2.prod_ref, bf16[8,2048,128]{2,1,0:T(8,128)(2,1)} %get-tuple-element.10.normed_ref, f32[128,1]{1,0:T(8,128)} %copy.11.gain_ref, f32[128,1]{1,0:T(8,128)} %copy.12.bias_ref, bf16[128,128]{1,0:T(8,128)(2,1)} %w_out_ref.1, bf16[128,128]{1,0:T(8,128)(2,1)} %w_gate_ref.1), custom_call_target="tpu_custom_call" | custom-call | tf_op jit(solution)/shard_map/leave/pallas_call | solution.py:152
Async XLA Ops:
  130.0 104.6 %all-to-all-start = ((bf16[128,8,2048]{2,1,0:T(8,128)(2,1)}), bf16[128,8,2048]{2,1,0:T(8,128)(2,1)}, u32[]{:S(2)}, u32[]{:S(2)}) async-start(bf16[128,8,2048]{2,1,0:T(8,128)(2,1)} %get-tuple-element.8), calls=%async_computation | async-start | bytes 8388608 | tf_op jit(solution)/shard_map/all_to_all | solution.py:180
  139.3 95.3 %collective-permute-start = (bf16[128,8,2048]{2,1,0:T(8,128)(2,1)}, bf16[128,8,2048]{2,1,0:T(8,128)(2,1)}, u32[]{:S(2)}, u32[]{:S(2)}) collective-permute-start(bf16[128,8,2048]{2,1,0:T(8,128)(2,1)} %all_to_all.15), channel_id=1, source_target_pairs={{0,4},{4,0},{1,5},{5,1},{2,6},{6,2},{3,7},{7,3},{8,12},{12,8},{9,1... | collective-permute-start | bytes 12582920 | tf_op jit(solution)/shard_map/ppermute | solution.py:179
  262.9 9.3 %copy-start = (f32[128]{0:T(128)S(1)}, f32[128]{0:T(128)}, u32[]{:S(2)}) copy-start(f32[128]{0:T(128)} %param.15) | copy-start | bytes 1540
  262.9 10.0 %copy-start.1 = (f32[128]{0:T(128)S(1)}, f32[128]{0:T(128)}, u32[]{:S(2)}) copy-start(f32[128]{0:T(128)} %param.16) | copy-start | bytes 1540
  262.9 104.6 %all-to-all-start.2 = ((bf16[128,8,2048]{2,1,0:T(8,128)(2,1)}), bf16[128,8,2048]{2,1,0:T(8,128)(2,1)}, u32[]{:S(2)}, u32[]{:S(2)}) async-start(bf16[128,8,2048]{2,1,0:T(8,128)(2,1)} %bitcast.11), calls=%async_computation.2 | async-start | bytes 8388608 | tf_op jit(solution)/shard_map/all_to_all | solution.py:188

commit v2 on v1

v2 whole, which is shorter than its diff:
```python
import functools

import jax
import jax.numpy as jnp
from jax import lax
from jax.experimental import pallas as pl
from jax.experimental.pallas import tpu as pltpu
from jax.sharding import Mesh
from jax.sharding import PartitionSpec as P

NZ, NY, NCORE, NX = 8, 4, 2, 4
CHIPS = ("z", "y", "x")
ROWS = 8
LANES = 128
VMEM_LIMIT = 56 * 1024 * 1024


def rows_norm(x, gain, bias):
    average = jnp.mean(x, axis=-1, keepdims=True)
    centred = x - average
    spread = jnp.mean(centred * centred, axis=-1, keepdims=True)
    return centred * lax.rsqrt(spread + 1e-05) * gain + bias


def sigmoid(x):
    return 0.5 * jnp.tanh(0.5 * x) + 0.5


def turned(w_ref, turned_ref):
    @pl.when(pl.program_id(0) == 0)
    def _():
        turned_ref[...] = w_ref[...].astype(jnp.float32).T.astype(jnp.bfloat16)

    return turned_ref


def gated(w_ref, normed, keep):
    hidden = w_ref.shape[0] // 2
    proj = lax.dot_general(
        w_ref[...], normed, (((1,), (1,)), ((), ())), preferred_element_type=jnp.float32
    )
    return sigmoid(proj[:hidden]) * proj[hidden:] * keep


def spread_rows(scr, i, value):
    for t in range(scr.shape[0]):
        part = value[:, t * LANES : (t + 1) * LANES]
        scr[t, pl.ds(i, value.shape[0], stride=ROWS), :] = part


def collect(scr, out_ref):
    hidden = out_ref.shape[0]
    for t in range(scr.shape[0]):
        block = scr[t].reshape(hidden, ROWS, LANES)
        out_ref[:, :, t * LANES : (t + 1) * LANES] = block.astype(jnp.bfloat16)


def enter_right_kernel(pair_ref, mask_ref, gain_ref, bias_ref, w_ref, right_ref, normed_ref, scr, w_scr):
    weights = turned(w_ref, w_scr)
    gain = gain_ref[...]
    bias = bias_ref[...]
    keep = mask_ref[...].astype(jnp.float32)
    for i in range(ROWS):
        normed = rows_norm(pair_ref[i].astype(jnp.float32), gain, bias).astype(jnp.bfloat16)
        normed_ref[i] = normed
        spread_rows(scr, i, gated(weights, normed, keep[i : i + 1]))
    collect(scr, right_ref)


def enter_left_kernel(normed_ref, mask_ref, w_ref, left_ref, scr, w_scr):
    weights = turned(w_ref, w_scr)
    keep = mask_ref[...].astype(jnp.float32)
    for i in range(ROWS):
        spread_rows(scr, i, gated(weights, normed_ref[i], keep[i : i + 1]))
    collect(scr, left_ref)


def whole(*shape):
    return pl.BlockSpec(shape, lambda *k: (0,) * len(shape))


def cost(flops, bytes_accessed, transcendentals=0):
    return pl.CostEstimate(
        flops=flops, bytes_accessed=bytes_accessed, transcendentals=transcendentals
    )


def enter(name, kernel, source, mask, weights, side_at, normed_too, first, columns, width=512):
    rows, total, channels = source.shape
    hidden = weights[-1].shape[1] // 4
    skip = first // width
    pair_spec = pl.BlockSpec((rows, width, channels), lambda k: (0, skip + k, 0))
    side_spec = pl.BlockSpec((hidden, rows, width), lambda k: (0, 0, k))
    side = jax.ShapeDtypeStruct((hidden, rows, columns), jnp.bfloat16)
    return pl.pallas_call(
        kernel,
        grid=(columns // width,),
        in_specs=[pair_spec, pl.BlockSpec((rows, width), lambda k: (0, skip + k))]
        + [whole(*w.shape) for w in weights[:-1]]
        + [pl.BlockSpec((channels, 2 * hidden), lambda k: (0, side_at))],
        out_specs=[side_spec, pair_spec] if normed_too else side_spec,
        out_shape=[side, jax.ShapeDtypeStruct(source.shape, jnp.bfloat16)] if normed_too else side,
        scratch_shapes=[
            pltpu.VMEM((width // LANES, hidden * rows, LANES), jnp.float32),
            pltpu.VMEM((2 * hidden, channels), jnp.bfloat16),
        ],
        compiler_params=pltpu.CompilerParams(vmem_limit_bytes=VMEM_LIMIT),
        cost_estimate=cost(4 * rows * columns * channels * hidden, 6 * rows * columns * channels, rows * columns * hidden),
        name=name,
    )(source, mask, *weights)


def product_kernel(own_steps, first_step, *refs):
    *a_refs, own_ref, other_ref, out_ref = refs

    def multiply(b_ref):
        total = None
        at = 0
        for a_ref in a_refs:
            depth = a_ref.shape[1]
            part = lax.dot_general(
                a_ref[...],
                b_ref[:, at : at + depth],
                (((1,), (1,)), ((), ())),
                preferred_element_type=jnp.float32,
            )
            total = part if total is None else total + part
            at += depth
        out_ref[...] = total.astype(jnp.bfloat16)

    first = pl.program_id(0) + first_step < own_steps
    pl.when(first)(lambda: multiply(own_ref))
    pl.when(jnp.logical_not(first))(lambda: multiply(other_ref))


def product(a_parts, own, other, first, columns, width=256):
    m = a_parts[0].shape[0]
    half, depth = own.shape
    steps, skip = half // width, first // width
    return pl.pallas_call(
        functools.partial(product_kernel, steps, skip),
        grid=(columns // width,),
        in_specs=[whole(*a.shape) for a in a_parts]
        + [
            pl.BlockSpec((width, depth), lambda k: (jnp.minimum(k + skip, steps - 1), 0)),
            pl.BlockSpec((width, depth), lambda k: (jnp.maximum(k + skip - steps, 0), 0)),
        ],
        out_specs=pl.BlockSpec((m, width), lambda k: (0, k)),
        out_shape=jax.ShapeDtypeStruct((m, columns), jnp.bfloat16),
        compiler_params=pltpu.CompilerParams(vmem_limit_bytes=VMEM_LIMIT),
        cost_estimate=cost(2 * m * depth * columns, 2 * m * depth + 2 * columns * depth + 2 * m * columns),
        name="product",
    )(*a_parts, own, other)


def leave_kernel(core_ref, prod_ref, normed_ref, gain_ref, bias_ref, w_out_ref, w_gate_ref, *refs):
    out_ref, scr = refs[-2:]
    hidden, rows, width = prod_ref.shape
    values = prod_ref[...].astype(jnp.float32)
    average = jnp.sum(values, axis=0, keepdims=True) * (1.0 / hidden)
    centred = values - average
    spread = jnp.sum(centred * centred, axis=0, keepdims=True) * (1.0 / hidden)
    scaled = centred * lax.rsqrt(spread + 1e-05)
    for t in range(width // LANES):
        scr[t] = scaled[:, :, t * LANES : (t + 1) * LANES].reshape(hidden * rows, LANES)
    gain = gain_ref[...]
    bias = bias_ref[...]
    for i in range(rows):
        values = [scr[t, pl.ds(i, hidden, stride=rows), :] for t in range(width // LANES)]
        post = (jnp.concatenate(values, axis=1) * gain + bias).astype(jnp.bfloat16)
        projected = lax.dot_general(
            post, w_out_ref[...], (((0,), (0,)), ((), ())), preferred_element_type=jnp.float32
        )
        normed = normed_ref[i].reshape(width, -1)
        gate = jnp.dot(normed, w_gate_ref[...], preferred_element_type=jnp.float32)
        out_ref[i] = (sigmoid(gate) * projected).astype(jnp.bfloat16).reshape(out_ref.shape[1:])


def leave(core, prod, normed, gain, bias, w_out, w_gate, first, before=None, width=512):
    hidden, rows, columns = prod.shape
    _, groups, _, part, channels = normed.shape
    count = width // part
    steps, skip = groups // count, first // width
    more = [] if before is None else [before]
    pair_spec = pl.BlockSpec(
        (rows, count, None, part, channels),
        lambda k, c: (0, lax.rem(k + skip, steps), jnp.where(k + skip < steps, c[0], 1 - c[0]), 0, 0),
    )
    return pl.pallas_call(
        leave_kernel,
        grid_spec=pltpu.PrefetchScalarGridSpec(
            num_scalar_prefetch=1,
            grid=(columns // width,),
            in_specs=[
                pl.BlockSpec((hidden, rows, width), lambda k, c: (0, 0, k)),
                pair_spec,
                whole(hidden, 1),
                whole(hidden, 1),
                whole(hidden, channels),
                whole(channels, channels),
            ]
            + [pl.BlockSpec(memory_space=pl.ANY)] * len(more),
            out_specs=pair_spec,
            scratch_shapes=[pltpu.VMEM((width // LANES, hidden * rows, LANES), jnp.float32)],
        ),
        out_shape=jax.ShapeDtypeStruct(normed.shape, jnp.bfloat16),
        input_output_aliases={7: 0} if more else {},
        compiler_params=pltpu.CompilerParams(vmem_limit_bytes=VMEM_LIMIT),
        cost_estimate=cost(4 * prod.size * channels, 6 * prod.size, prod.size),
        name="leave",
    )(core, prod, normed, gain, bias, w_out, w_gate, *more)


def shards(pair, pair_mask, in_gain, in_bias, w_proj, w_gate, out_gain, out_bias, w_out):
    rows, total, channels = pair.shape
    hidden = w_out.shape[0]
    right, normed = enter(
        "enter_right",
        enter_right_kernel,
        pair,
        pair_mask,
        (in_gain.reshape(1, -1), in_bias.reshape(1, -1), w_proj),
        1,
        True,
        0,
        total,
    )
    enter_left = functools.partial(
        enter, "enter_left", enter_left_kernel, normed, pair_mask, (w_proj,), 0, False
    )
    exchange = functools.partial(lax.all_to_all, axis_name=CHIPS, split_axis=0, concat_axis=0, tiled=True)
    matrix = (hidden * rows, -1)
    own = exchange(right)
    other = lax.ppermute(own, "core", [(0, 1), (1, 0)])
    a_parts = [exchange(enter_left(0, total)).reshape(matrix)]
    core = lax.axis_index("core").reshape(1)
    normed = normed.reshape(rows, NZ * NY, NCORE, NX * rows, channels)
    vectors = (out_gain.reshape(-1, 1), out_bias.reshape(-1, 1), w_out, w_gate)
    own, other = own.reshape(matrix), other.reshape(matrix)
    rest = product(a_parts, own, other, 0, total).reshape(hidden, rows, -1)
    out = leave(core, exchange(rest), normed, *vectors, 0)
    return out.reshape(pair.shape)


def solution(mesh):
    fine = Mesh(mesh.devices.reshape(NZ, NY, NCORE, NX), ("z", "y", "core", "x"))
    split = ("z", "y", "core", "x")
    return jax.shard_map(
        shards,
        mesh=fine,
        in_specs=(P(split), P(split), P(), P(), P(), P(), P(), P(), P()),
        out_specs=P(split),
        check_vma=False,
    )
```

time: 379 us -> 358 us (0.945)
  blocking collectives: 111 us -> 0 us
  waiting for transfers between devices: 189 us -> 277 us
  starting transfers between devices: 18.7 us -> 34.6 us
  Pallas kernels: 56.5 us -> 43.8 us
    all_to_all x1 -> x0, blocking collectives: 111 us -> none  [shards(): own = exchange(right)]
    all_to_all x2 -> x3, waiting for transfers between devices: 189 us -> 277 us  [the longest x1 95.2 us: shards(): a_parts = [exchange(enter_left(0, total)).reshape(matrix)]]
    all_to_all x2 -> x3, starting transfers between devices: 18.6 us -> 34.5 us  [the longest x1 15.8 us: shards(): own = exchange(right)]
    pallas_call x3 -> x4, Pallas kernels: 56.5 us -> 43.8 us  [the longest x2 19.5 us: enter(): pl.pallas_call(kernel, grid=(columns // width,), in_specs=[pair_spec, pl....]
  transfers between devices with their start and end apart: 3 -> 4, of which waited for: 2 -> 3; matrix products, arithmetic and copies ran while one was open for 0% -> 0% of each run, Pallas kernels for 0% -> 2%
where the time goes in v2:
time: 358 us; the launch traced here: 357 us
  waiting for transfers between devices  277 us (77%)
  Pallas kernels  43.8 us (12%)
  starting transfers between devices  34.6 us (10%)
    all_to_all x1, waiting for transfers between devices, shards(): a_parts = [exchange(enter_left(0, total)).reshape(matrix)]  95.2 us
    all_to_all x1, waiting for transfers between devices, shards(): out = leave(core, exchange(rest), normed, *vectors, 0)  93.8 us
    all_to_all x1, waiting for transfers between devices, shards(): own = exchange(right)  87.9 us
    pallas_call x2, Pallas kernels, enter(): pl.pallas_call(kernel, grid=(columns // width,), in_specs=[pair_spec, pl....  19.5 us
    all_to_all x1, starting transfers between devices, shards(): own = exchange(right)  15.8 us
    pallas_call x1, Pallas kernels, product(): pl.pallas_call(functools.partial(product_kernel, steps, skip), grid=(colu...  14.4 us
    pallas_call x1, Pallas kernels, leave(): pl.pallas_call(leave_kernel, grid_spec=pltpu.PrefetchScalarGridSpec(num_s...  9.92 us
    all_to_all x1, starting transfers between devices, shards(): out = leave(core, exchange(rest), normed, *vectors, 0)  9.4 us
  transfers between devices with their start and end apart: 4, of which 3 were waited for; matrix products, arithmetic and copies ran while one was open for 0% of the time, Pallas kernels for 2%

profile of v2, /device:TPU:6, one launch (start us, length us, event | category | flops | bytes accessed | tf_op | source)
XLA Modules:
  0.0 356.9 jit_solution(8895507371945422680)
XLA Ops:
  0.0 11.8 %enter_right.1 = (bf16[128,8,2048]{2,1,0:T(8,128)(2,1)}, bf16[8,2048,128]{2,1,0:T(8,128)(2,1)}) custom-call(bf16[8,2048,128]{2,1,0:T(8,128)(2,1)} %pair_ref.1, s32[8,2048]{1,0:T(8,128)} %mask_ref.3, f32[1,128]{1,0:T(1,128)} %bitcast.13, f32[1,128]{1,0:T(1,128)} %bitcast.14, bf16[128,512]{1,0:T(8,128)(2,1)} %w_ref.3), custom_call_target="tpu_custom_call" | custom-call | flops 1073741824 | bytes 12582912 | tf_op jit(solution)/shard_map/enter_right/pallas_call | solution.py:95
  11.8 15.8 %all-to-all-start.1 = ((bf16[128,8,2048]{2,1,0:T(8,128)(2,1)}), bf16[128,8,2048]{2,1,0:T(8,128)(2,1)}, u32[]{:S(2)}, u32[]{:S(2)}) async-start(bf16[128,8,2048]{2,1,0:T(8,128)(2,1)} %get-tuple-element.8), calls=%async_computation.1 | async-start | bytes 8388608 | tf_op jit(solution)/shard_map/all_to_all | solution.py:233
  27.7 7.6 %enter_left.1 = bf16[128,8,2048]{2,1,0:T(8,128)(2,1)} custom-call(bf16[8,2048,128]{2,1,0:T(8,128)(2,1)} %get-tuple-element.7.normed_ref, s32[8,2048]{1,0:T(8,128)} %mask_ref.3, bf16[128,512]{1,0:T(8,128)(2,1)} %w_ref.3), custom_call_target="tpu_custom_call" | custom-call | flops 1073741824 | bytes 12582912 | tf_op jit(solution)/shard_map/enter_left/pallas_call | solution.py:95
  35.3 87.9 %all-to-all-done.1 = bf16[128,8,2048]{2,1,0:T(8,128)(2,1)} async-done(((bf16[128,8,2048]{2,1,0:T(8,128)(2,1)}), bf16[128,8,2048]{2,1,0:T(8,128)(2,1)}, u32[]{:S(2)}, u32[]{:S(2)}) %all-to-all-start.1) | async-done | bytes 4194336 | tf_op jit(solution)/shard_map/all_to_all | solution.py:233
  123.2 9.3 %all-to-all-start = ((bf16[128,8,2048]{2,1,0:T(8,128)(2,1)}), bf16[128,8,2048]{2,1,0:T(8,128)(2,1)}, u32[]{:S(2)}, u32[]{:S(2)}) async-start(bf16[128,8,2048]{2,1,0:T(8,128)(2,1)} %enter_left.1), calls=%async_computation | async-start | bytes 8388608 | tf_op jit(solution)/shard_map/all_to_all | solution.py:235
  132.5 0.1 collective-permute-start
  132.6 95.2 %all-to-all-done = bf16[128,8,2048]{2,1,0:T(8,128)(2,1)} async-done(((bf16[128,8,2048]{2,1,0:T(8,128)(2,1)}), bf16[128,8,2048]{2,1,0:T(8,128)(2,1)}, u32[]{:S(2)}, u32[]{:S(2)}) %all-to-all-start) | async-done | bytes 4194336 | tf_op jit(solution)/shard_map/all_to_all | solution.py:235
  227.8 0.0 collective-permute-done
  227.8 14.4 %product.1 = bf16[1024,2048]{1,0:T(8,128)(2,1)} custom-call(bf16[1024,2048]{1,0:T(8,128)(2,1)} %bitcast.3.refs_0_, bf16[1024,2048]{1,0:T(8,128)(2,1)} %bitcast.4.refs_1_, bf16[1024,2048]{1,0:T(8,128)(2,1)} %bitcast.5.refs_2_), custom_call_target="tpu_custom_call" | custom-call | flops 8589934592 | bytes 16777216 | tf_op jit(solution)/shard_map/product/pallas_call | solution.py:140
  242.3 0.0 copy-start
  242.3 0.0 copy-start.1
  242.3 9.4 %all-to-all-start.2 = ((bf16[128,8,2048]{2,1,0:T(8,128)(2,1)}), bf16[128,8,2048]{2,1,0:T(8,128)(2,1)}, u32[]{:S(2)}, u32[]{:S(2)}) async-start(bf16[128,8,2048]{2,1,0:T(8,128)(2,1)} %bitcast.12), calls=%async_computation.2 | async-start | bytes 8388608 | tf_op jit(solution)/shard_map/all_to_all | solution.py:241
  251.7 0.0 copy-done
  251.7 0.7 copy.10.gain_ref
  252.4 0.0 copy-done.1
  252.4 0.7 copy.11.bias_ref
  253.2 93.8 %all-to-all-done.2.prod_ref = bf16[128,8,2048]{2,1,0:T(8,128)(2,1)} async-done(((bf16[128,8,2048]{2,1,0:T(8,128)(2,1)}), bf16[128,8,2048]{2,1,0:T(8,128)(2,1)}, u32[]{:S(2)}, u32[]{:S(2)}) %all-to-all-start.2) | async-done | bytes 4194336 | tf_op jit(solution)/shard_map/all_to_all | solution.py:241
  347.0 9.9 %leave.1 = bf16[8,32,2,32,128]{4,3,2,1,0:T(8,128)(2,1)} custom-call(s32[1]{0:T(128)} %bitcast.core_ref, bf16[128,8,2048]{2,1,0:T(8,128)(2,1)} %all-to-all-done.2.prod_ref, bf16[8,32,2,32,128]{4,3,2,1,0:T(8,128)(2,1)} %bitcast.11, f32[128,1]{1,0:T(8,128)} %copy.10.gain_ref, f32[128,1]{1,0:T(8,128)} %copy.11.bias_ref, bf16[128,128]{1,0:T(8,128)(2,1)} %w_out_ref.1, ...), custom_call_target="tpu_custom_call" | custom-call | flops 1073741824 | bytes 12582912 | tf_op jit(solution)/shard_map/leave/pallas_call | solution.py:189
Async XLA Ops:
  11.8 111.4 %all-to-all-start.1 = ((bf16[128,8,2048]{2,1,0:T(8,128)(2,1)}), bf16[128,8,2048]{2,1,0:T(8,128)(2,1)}, u32[]{:S(2)}, u32[]{:S(2)}) async-start(bf16[128,8,2048]{2,1,0:T(8,128)(2,1)} %get-tuple-element.8), calls=%async_computation.1 | async-start | bytes 8388608 | tf_op jit(solution)/shard_map/all_to_all | solution.py:233
  123.2 104.6 %all-to-all-start = ((bf16[128,8,2048]{2,1,0:T(8,128)(2,1)}), bf16[128,8,2048]{2,1,0:T(8,128)(2,1)}, u32[]{:S(2)}, u32[]{:S(2)}) async-start(bf16[128,8,2048]{2,1,0:T(8,128)(2,1)} %enter_left.1), calls=%async_computation | async-start | bytes 8388608 | tf_op jit(solution)/shard_map/all_to_all | solution.py:235
  132.5 95.3 %collective-permute-start = (bf16[128,8,2048]{2,1,0:T(8,128)(2,1)}, bf16[128,8,2048]{2,1,0:T(8,128)(2,1)}, u32[]{:S(2)}, u32[]{:S(2)}) collective-permute-start(bf16[128,8,2048]{2,1,0:T(8,128)(2,1)} %all-to-all-done.1), channel_id=1, source_target_pairs={{0,4},{4,0},{1,5},{5,1},{2,6},{6,2},{3,7},{7,3},{8,12},{12,8},{9,1... | collective-permute-start | bytes 12582920 | tf_op jit(solution)/shard_map/ppermute | solution.py:234
  242.3 9.4 %copy-start = (f32[128]{0:T(128)S(1)}, f32[128]{0:T(128)}, u32[]{:S(2)}) copy-start(f32[128]{0:T(128)} %param.15) | copy-start | bytes 1540
  242.3 10.2 %copy-start.1 = (f32[128]{0:T(128)S(1)}, f32[128]{0:T(128)}, u32[]{:S(2)}) copy-start(f32[128]{0:T(128)} %param.16) | copy-start | bytes 1540
  242.3 104.7 %all-to-all-start.2 = ((bf16[128,8,2048]{2,1,0:T(8,128)(2,1)}), bf16[128,8,2048]{2,1,0:T(8,128)(2,1)}, u32[]{:S(2)}, u32[]{:S(2)}) async-start(bf16[128,8,2048]{2,1,0:T(8,128)(2,1)} %bitcast.12), calls=%async_computation.2 | async-start | bytes 8388608 | tf_op jit(solution)/shard_map/all_to_all | solution.py:241

commit v3 on v2

v3 whole, which is shorter than its diff:
```python
import functools

import jax
import jax.numpy as jnp
from jax import lax
from jax.experimental import pallas as pl
from jax.experimental.pallas import tpu as pltpu
from jax.sharding import Mesh
from jax.sharding import PartitionSpec as P

NZ, NY, NCORE, NX = 8, 4, 2, 4
CHIPS = ("z", "y", "x")
ROWS = 8
LANES = 128
MIB = 1024 * 1024
VMEM_LIMIT = 56 * MIB


def rows_norm(x, gain, bias):
    average = jnp.mean(x, axis=-1, keepdims=True)
    centred = x - average
    spread = jnp.mean(centred * centred, axis=-1, keepdims=True)
    return centred * lax.rsqrt(spread + 1e-05) * gain + bias


def sigmoid(x):
    return 0.5 * jnp.tanh(0.5 * x) + 0.5


def turned(w_ref, turned_ref):
    @pl.when(pl.program_id(0) == 0)
    def _():
        turned_ref[...] = w_ref[...].astype(jnp.float32).T.astype(jnp.bfloat16)

    return turned_ref


def gated(w_ref, normed, keep):
    hidden = w_ref.shape[0] // 2
    proj = lax.dot_general(
        w_ref[...], normed, (((1,), (1,)), ((), ())), preferred_element_type=jnp.float32
    )
    return sigmoid(proj[:hidden]) * proj[hidden:] * keep


def spread_rows(scr, i, value):
    for t in range(scr.shape[0]):
        part = value[:, t * LANES : (t + 1) * LANES]
        scr[t, pl.ds(i, value.shape[0], stride=ROWS), :] = part


def collect(scr, out_ref):
    hidden = out_ref.shape[0]
    for t in range(scr.shape[0]):
        block = scr[t].reshape(hidden, ROWS, LANES)
        out_ref[:, :, t * LANES : (t + 1) * LANES] = block.astype(jnp.bfloat16)


def enter_kernel(pair_ref, mask_ref, gain_ref, bias_ref, w_ref, side_ref, *refs):
    *normed_refs, scr, w_scr = refs
    weights = turned(w_ref, w_scr)
    keep = mask_ref[...].astype(jnp.float32)
    rows, width, channels = pair_ref.shape
    values = pair_ref[...].reshape(rows * width, channels).astype(jnp.float32)
    normed = rows_norm(values, gain_ref[...], bias_ref[...]).astype(jnp.bfloat16)
    for i in range(rows):
        part = normed[i * width : (i + 1) * width]
        for normed_ref in normed_refs:
            normed_ref[i] = part
        spread_rows(scr, i, gated(weights, part, keep[i : i + 1]))
    collect(scr, side_ref)


def whole(*shape):
    return pl.BlockSpec(shape, lambda *k: (0,) * len(shape))


def cost(flops, bytes_accessed, transcendentals=0):
    return pl.CostEstimate(
        flops=flops, bytes_accessed=bytes_accessed, transcendentals=transcendentals
    )


def enter(name, pair, mask, gain, bias, w_proj, side_at, normed_too, width=512):
    rows, total, channels = pair.shape
    hidden = w_proj.shape[1] // 4
    pair_spec = pl.BlockSpec((rows, width, channels), lambda k: (0, k, 0))
    side = jax.ShapeDtypeStruct((hidden, rows, total), jnp.bfloat16)
    return pl.pallas_call(
        enter_kernel,
        grid=(total // width,),
        in_specs=[
            pair_spec,
            pl.BlockSpec((rows, width), lambda k: (0, k)),
            whole(1, channels),
            whole(1, channels),
            pl.BlockSpec((channels, 2 * hidden), lambda k: (0, side_at)),
        ],
        out_specs=[pl.BlockSpec((hidden, rows, width), lambda k: (0, 0, k))] + [pair_spec] * normed_too,
        out_shape=[side] + [jax.ShapeDtypeStruct(pair.shape, jnp.bfloat16)] * normed_too,
        scratch_shapes=[
            pltpu.VMEM((width // LANES, hidden * rows, LANES), jnp.float32),
            pltpu.VMEM((2 * hidden, channels), jnp.bfloat16),
        ],
        compiler_params=pltpu.CompilerParams(vmem_limit_bytes=VMEM_LIMIT),
        cost_estimate=cost(4 * pair.size * hidden, 6 * pair.size, pair.size),
        name=name,
    )(pair, mask, gain, bias, w_proj)


def product_kernel(own_steps, a_ref, own_ref, other_ref, out_ref):
    def multiply(b_ref):
        out_ref[...] = lax.dot_general(
            a_ref[...],
            b_ref[...],
            (((1,), (1,)), ((), ())),
            preferred_element_type=jnp.float32,
        ).astype(jnp.bfloat16)

    step = pl.program_id(0)
    pl.when(step < own_steps)(lambda: multiply(own_ref))
    pl.when(step >= own_steps)(lambda: multiply(other_ref))


def product(a, own, other, width=512):
    m, depth = a.shape
    half = own.shape[0]
    steps = half // width
    return pl.pallas_call(
        functools.partial(product_kernel, steps),
        grid=(2 * steps,),
        in_specs=[
            whole(m, depth),
            pl.BlockSpec((width, depth), lambda k: (jnp.minimum(k, steps - 1), 0)),
            pl.BlockSpec((width, depth), lambda k: (jnp.maximum(k - steps, 0), 0)),
        ],
        out_specs=pl.BlockSpec((m, width), lambda k: (0, k)),
        out_shape=jax.ShapeDtypeStruct((m, 2 * half), jnp.bfloat16),
        compiler_params=pltpu.CompilerParams(vmem_limit_bytes=VMEM_LIMIT),
        cost_estimate=cost(4 * m * depth * half, 2 * (m * depth + 2 * half * depth + 2 * m * half)),
        name="product",
    )(a, own, other)


def leave_kernel(core_ref, prod_ref, normed_ref, gain_ref, bias_ref, w_ref, out_ref, scr):
    hidden, rows, width = prod_ref.shape
    channels = normed_ref.shape[-1]
    values = prod_ref[...].astype(jnp.float32)
    average = jnp.sum(values, axis=0, keepdims=True) * (1.0 / hidden)
    centred = values - average
    spread = jnp.sum(centred * centred, axis=0, keepdims=True) * (1.0 / hidden)
    scaled = centred * lax.rsqrt(spread + 1e-05)
    for t in range(width // LANES):
        scr[t] = scaled[:, :, t * LANES : (t + 1) * LANES].reshape(hidden * rows, LANES)
    gain = gain_ref[...]
    bias = bias_ref[...]
    for i in range(rows):
        post = jnp.concatenate(
            [
                (scr[t, pl.ds(i, hidden, stride=rows), :].T * gain + bias).astype(jnp.bfloat16)
                for t in range(width // LANES)
            ],
            axis=0,
        )
        normed = normed_ref[i].reshape(width, channels)
        result = jnp.dot(
            jnp.concatenate([post, normed], axis=1), w_ref[...], preferred_element_type=jnp.float32
        )
        update = sigmoid(result[:, channels:]) * result[:, :channels]
        out_ref[i] = update.astype(jnp.bfloat16).reshape(out_ref.shape[1:])


def leave(core, prod, normed, gain, bias, w, width=512):
    hidden, rows, columns = prod.shape
    _, groups, _, part, channels = normed.shape
    count = width // part
    steps = groups // count
    pair_spec = pl.BlockSpec(
        (rows, count, None, part, channels),
        lambda k, c: (0, lax.rem(k, steps), jnp.where(k < steps, c[0], 1 - c[0]), 0, 0),
    )
    return pl.pallas_call(
        leave_kernel,
        grid_spec=pltpu.PrefetchScalarGridSpec(
            num_scalar_prefetch=1,
            grid=(columns // width,),
            in_specs=[
                pl.BlockSpec((hidden, rows, width), lambda k, c: (0, 0, k)),
                pair_spec,
                whole(1, hidden),
                whole(1, hidden),
                whole(*w.shape),
            ],
            out_specs=pair_spec,
            scratch_shapes=[pltpu.VMEM((width // LANES, hidden * rows, LANES), jnp.float32)],
        ),
        out_shape=jax.ShapeDtypeStruct(normed.shape, jnp.bfloat16),
        compiler_params=pltpu.CompilerParams(vmem_limit_bytes=VMEM_LIMIT),
        cost_estimate=cost(4 * prod.size * channels, 6 * prod.size, prod.size),
        name="leave",
    )(core, prod, normed, gain, bias, w)


def shards(pair, pair_mask, in_gain, in_bias, w_proj, w_gate, out_gain, out_bias, w_out):
    rows, total, channels = pair.shape
    hidden = w_out.shape[0]
    given = (pair, pair_mask, in_gain.reshape(1, -1), in_bias.reshape(1, -1), w_proj)
    (right,) = enter("enter_right", *given, 1, False)
    left, normed = enter("enter_left", *given, 0, True)
    exchange = functools.partial(lax.all_to_all, axis_name=CHIPS, split_axis=0, concat_axis=0, tiled=True)
    matrix = (hidden * rows, total)
    own = exchange(right)
    other = lax.ppermute(own, "core", [(0, 1), (1, 0)])
    prod = product(exchange(left).reshape(matrix), own.reshape(matrix), other.reshape(matrix))
    back = exchange(prod.reshape(hidden, rows, total))
    w_both = jnp.zeros((hidden + channels, 2 * channels), jnp.bfloat16)
    w_both = w_both.at[:hidden, :channels].set(w_out).at[hidden:, channels:].set(w_gate)
    out = leave(
        lax.axis_index("core").reshape(1),
        back,
        normed.reshape(rows, NZ * NY, NCORE, NX * rows, channels),
        out_gain.reshape(1, -1),
        out_bias.reshape(1, -1),
        w_both,
    )
    return out.reshape(pair.shape)


def solution(mesh):
    fine = Mesh(mesh.devices.reshape(NZ, NY, NCORE, NX), ("z", "y", "core", "x"))
    split = ("z", "y", "core", "x")
    return jax.shard_map(
        shards,
        mesh=fine,
        in_specs=(P(split), P(split), P(), P(), P(), P(), P(), P(), P()),
        out_specs=P(split),
        check_vma=False,
    )
```

time: 358 us -> 355 us (level)
    all_to_all x1, waiting for transfers between devices: 87.9 us -> 84.1 us  [shards(): own = exchange(right)]
  transfers between devices with their start and end apart: 4 -> 4, of which waited for: 3 -> 3; matrix products, arithmetic and copies ran while one was open for 0% -> 0% of each run, Pallas kernels for 2% -> 3%
where the time goes in v3:
time: 355 us
  waiting for transfers between devices  274 us (77%)
  Pallas kernels  45.6 us (13%)
  starting transfers between devices  34.8 us (10%)
    all_to_all x1, waiting for transfers between devices, shards(): back = exchange(prod.reshape(hidden, rows, total))  95.2 us
    all_to_all x1, waiting for transfers between devices, shards(): exchange(left).reshape(matrix)  95 us
    all_to_all x1, waiting for transfers between devices, shards(): own = exchange(right)  84.1 us
    pallas_call x2, Pallas kernels, enter(): pl.pallas_call(enter_kernel, grid=(total // width,), in_specs=[pair_spec,...  22.4 us
    all_to_all x1, starting transfers between devices, shards(): own = exchange(right)  15.8 us
    pallas_call x1, Pallas kernels, product(): pl.pallas_call(functools.partial(product_kernel, steps), grid=(2 * steps,...  14 us
    all_to_all x1, starting transfers between devices, shards(): back = exchange(prod.reshape(hidden, rows, total))  9.39 us
    all_to_all x1, starting transfers between devices, shards(): exchange(left).reshape(matrix)  9.31 us
  transfers between devices with their start and end apart: 4, of which 3 were waited for; matrix products, arithmetic and copies ran while one was open for 0% of the time, Pallas kernels for 3%

profile of v3, /device:TPU:6, one launch (start us, length us, event | category | flops | bytes accessed | tf_op | source)
XLA Modules:
  0.0 354.9 jit_solution(16027368334185592328)
XLA Ops:
  0.0 11.0 %enter_right.1 = bf16[128,8,2048]{2,1,0:T(8,128)(2,1)} custom-call(bf16[8,2048,128]{2,1,0:T(8,128)(2,1)} %pair_ref.3, s32[8,2048]{1,0:T(8,128)} %mask_ref.3, f32[1,128]{1,0:T(1,128)} %bitcast.13, f32[1,128]{1,0:T(1,128)} %bitcast.15, bf16[128,512]{1,0:T(8,128)(2,1)} %w_ref.3), custom_call_target="tpu_custom_call" | custom-call | flops 1073741824 | bytes 12582912 | tf_op jit(solution)/shard_map/enter_right/pallas_call | solution.py:89
  11.0 15.8 %all-to-all-start.1 = ((bf16[128,8,2048]{2,1,0:T(8,128)(2,1)}), bf16[128,8,2048]{2,1,0:T(8,128)(2,1)}, u32[]{:S(2)}, u32[]{:S(2)}) async-start(bf16[128,8,2048]{2,1,0:T(8,128)(2,1)} %enter_right.1), calls=%async_computation.1 | async-start | bytes 8388608 | tf_op jit(solution)/shard_map/all_to_all | solution.py:212
  26.8 11.4 %enter_left.1 = (bf16[128,8,2048]{2,1,0:T(8,128)(2,1)}, bf16[8,2048,128]{2,1,0:T(8,128)(2,1)}) custom-call(bf16[8,2048,128]{2,1,0:T(8,128)(2,1)} %pair_ref.3, s32[8,2048]{1,0:T(8,128)} %mask_ref.3, f32[1,128]{1,0:T(1,128)} %bitcast.14, f32[1,128]{1,0:T(1,128)} %bitcast.16, bf16[128,512]{1,0:T(8,128)(2,1)} %w_ref.3), custom_call_target="tpu_custom_call" | custom-call | flops 1073741824 | bytes 12582912 | tf_op jit(solution)/shard_map/enter_left/pallas_call | solution.py:89
  38.2 84.1 %all-to-all-done.1 = bf16[128,8,2048]{2,1,0:T(8,128)(2,1)} async-done(((bf16[128,8,2048]{2,1,0:T(8,128)(2,1)}), bf16[128,8,2048]{2,1,0:T(8,128)(2,1)}, u32[]{:S(2)}, u32[]{:S(2)}) %all-to-all-start.1) | async-done | bytes 4194336 | tf_op jit(solution)/shard_map/all_to_all | solution.py:212
  122.4 9.3 %all-to-all-start = ((bf16[128,8,2048]{2,1,0:T(8,128)(2,1)}), bf16[128,8,2048]{2,1,0:T(8,128)(2,1)}, u32[]{:S(2)}, u32[]{:S(2)}) async-start(bf16[128,8,2048]{2,1,0:T(8,128)(2,1)} %get-tuple-element.31), calls=%async_computation | async-start | bytes 8388608 | tf_op jit(solution)/shard_map/all_to_all | solution.py:214
  131.7 0.3 collective-permute-start
  132.0 95.0 %all-to-all-done = bf16[128,8,2048]{2,1,0:T(8,128)(2,1)} async-done(((bf16[128,8,2048]{2,1,0:T(8,128)(2,1)}), bf16[128,8,2048]{2,1,0:T(8,128)(2,1)}, u32[]{:S(2)}, u32[]{:S(2)}) %all-to-all-start) | async-done | bytes 4194336 | tf_op jit(solution)/shard_map/all_to_all | solution.py:214
  227.0 0.0 collective-permute-done
  227.0 14.0 %product.1 = bf16[1024,2048]{1,0:T(8,128)(2,1)} custom-call(bf16[1024,2048]{1,0:T(8,128)(2,1)} %bitcast.3.a_ref, bf16[1024,2048]{1,0:T(8,128)(2,1)} %bitcast.4.own_ref, bf16[1024,2048]{1,0:T(8,128)(2,1)} %bitcast.5.other_ref), custom_call_target="tpu_custom_call" | custom-call | flops 8589934592 | bytes 16777216 | tf_op jit(solution)/shard_map/product/pallas_call | solution.py:129
  241.0 0.0 copy-start.1
  241.0 0.0 copy-start.2
  241.0 9.4 %all-to-all-start.2 = ((bf16[128,8,2048]{2,1,0:T(8,128)(2,1)}), bf16[128,8,2048]{2,1,0:T(8,128)(2,1)}, u32[]{:S(2)}, u32[]{:S(2)}) async-start(bf16[128,8,2048]{2,1,0:T(8,128)(2,1)} %bitcast.12), calls=%async_computation.2 | async-start | bytes 8388608 | tf_op jit(solution)/shard_map/all_to_all | solution.py:215
  250.4 0.0 copy-done.1
  250.5 0.0 copy-done.2
  250.5 0.0 copy-start
  250.5 95.2 %all-to-all-done.2.prod_ref = bf16[128,8,2048]{2,1,0:T(8,128)(2,1)} async-done(((bf16[128,8,2048]{2,1,0:T(8,128)(2,1)}), bf16[128,8,2048]{2,1,0:T(8,128)(2,1)}, u32[]{:S(2)}, u32[]{:S(2)}) %all-to-all-start.2) | async-done | bytes 4194336 | tf_op jit(solution)/shard_map/all_to_all | solution.py:215
  345.7 0.0 copy-done
  345.7 9.2 %leave.1 = bf16[8,32,2,32,128]{4,3,2,1,0:T(8,128)(2,1)} custom-call(s32[1]{0:T(128)} %bitcast.core_ref, bf16[128,8,2048]{2,1,0:T(8,128)(2,1)} %all-to-all-done.2.prod_ref, bf16[8,32,2,32,128]{4,3,2,1,0:T(8,128)(2,1)} %bitcast.11, f32[1,128]{1,0:T(1,128)} %bitcast.17, f32[1,128]{1,0:T(1,128)} %bitcast.18, bf16[256,256]{1,0:T(8,128)(2,1)} %copy-done), custom_call_target="tpu_custom_call" | custom-call | flops 1073741824 | bytes 12582912 | tf_op jit(solution)/shard_map/leave/pallas_call | solution.py:182
  (2 shorter events, 0.0 us)
Async XLA Ops:
  11.0 111.4 %all-to-all-start.1 = ((bf16[128,8,2048]{2,1,0:T(8,128)(2,1)}), bf16[128,8,2048]{2,1,0:T(8,128)(2,1)}, u32[]{:S(2)}, u32[]{:S(2)}) async-start(bf16[128,8,2048]{2,1,0:T(8,128)(2,1)} %enter_right.1), calls=%async_computation.1 | async-start | bytes 8388608 | tf_op jit(solution)/shard_map/all_to_all | solution.py:212
  122.4 104.6 %all-to-all-start = ((bf16[128,8,2048]{2,1,0:T(8,128)(2,1)}), bf16[128,8,2048]{2,1,0:T(8,128)(2,1)}, u32[]{:S(2)}, u32[]{:S(2)}) async-start(bf16[128,8,2048]{2,1,0:T(8,128)(2,1)} %get-tuple-element.31), calls=%async_computation | async-start | bytes 8388608 | tf_op jit(solution)/shard_map/all_to_all | solution.py:214
  131.7 95.3 %collective-permute-start = (bf16[128,8,2048]{2,1,0:T(8,128)(2,1)}, bf16[128,8,2048]{2,1,0:T(8,128)(2,1)}, u32[]{:S(2)}, u32[]{:S(2)}) collective-permute-start(bf16[128,8,2048]{2,1,0:T(8,128)(2,1)} %all-to-all-done.1), channel_id=1, source_target_pairs={{0,4},{4,0},{1,5},{5,1},{2,6},{6,2},{3,7},{7,3},{8,12},{12,8},{9,1... | collective-permute-start | bytes 12582920 | tf_op jit(solution)/shard_map/ppermute | solution.py:213
  241.0 9.4 %copy-start.1 = (bf16[128,128]{1,0:T(8,128)(2,1)S(1)}, bf16[128,128]{1,0:T(8,128)(2,1)}, u32[]{:S(2)}) copy-start(bf16[128,128]{1,0:T(8,128)(2,1)} %param.21) | copy-start | bytes 98308
  241.0 9.4 %copy-start.2 = (bf16[128,128]{1,0:T(8,128)(2,1)S(1)}, bf16[128,128]{1,0:T(8,128)(2,1)}, u32[]{:S(2)}) copy-start(bf16[128,128]{1,0:T(8,128)(2,1)} %param.18) | copy-start | bytes 98308
  241.0 104.7 %all-to-all-start.2 = ((bf16[128,8,2048]{2,1,0:T(8,128)(2,1)}), bf16[128,8,2048]{2,1,0:T(8,128)(2,1)}, u32[]{:S(2)}, u32[]{:S(2)}) async-start(bf16[128,8,2048]{2,1,0:T(8,128)(2,1)} %bitcast.12), calls=%async_computation.2 | async-start | bytes 8388608 | tf_op jit(solution)/shard_map/all_to_all | solution.py:215
  250.5 95.3 %copy-start = (bf16[256,256]{1,0:T(8,128)(2,1)}, bf16[256,256]{1,0:T(8,128)(2,1)S(1)}, u32[]{:S(2)}) copy-start(bf16[256,256]{1,0:T(8,128)(2,1)S(1)} %constant_dynamic-update-slice_fusion.w_ref) | copy-start | bytes 393220

commit v4 on v3

--- a/solution.py
+++ b/solution.py
@@ -23,14 +23,14 @@
     return centred * lax.rsqrt(spread + 1e-05) * gain + bias
 
 
-def sigmoid(x):
-    return 0.5 * jnp.tanh(0.5 * x) + 0.5
+def gate_by(half_gate, half_value):
+    return (jnp.tanh(half_gate) + 1.0) * half_value
 
 
 def turned(w_ref, turned_ref):
     @pl.when(pl.program_id(0) == 0)
     def _():
-        turned_ref[...] = w_ref[...].astype(jnp.float32).T.astype(jnp.bfloat16)
+        turned_ref[...] = (w_ref[...].astype(jnp.float32).T * 0.5).astype(jnp.bfloat16)
 
     return turned_ref
 
@@ -40,7 +40,7 @@
     proj = lax.dot_general(
         w_ref[...], normed, (((1,), (1,)), ((), ())), preferred_element_type=jnp.float32
     )
-    return sigmoid(proj[:hidden]) * proj[hidden:] * keep
+    return gate_by(proj[:hidden], proj[hidden:] * keep)
 
 
 def spread_rows(scr, i, value):
@@ -166,7 +166,7 @@
         result = jnp.dot(
             jnp.concatenate([post, normed], axis=1), w_ref[...], preferred_element_type=jnp.float32
         )
-        update = sigmoid(result[:, channels:]) * result[:, :channels]
+        update = gate_by(result[:, channels:], result[:, :channels])
         out_ref[i] = update.astype(jnp.bfloat16).reshape(out_ref.shape[1:])
 
 
@@ -214,7 +214,7 @@
     prod = product(exchange(left).reshape(matrix), own.reshape(matrix), other.reshape(matrix))
     back = exchange(prod.reshape(hidden, rows, total))
     w_both = jnp.zeros((hidden + channels, 2 * channels), jnp.bfloat16)
-    w_both = w_both.at[:hidden, :channels].set(w_out).at[hidden:, channels:].set(w_gate)
+    w_both = w_both.at[:hidden, :channels].set(w_out * 0.5).at[hidden:, channels:].set(w_gate * 0.5)
     out = leave(
         lax.axis_index("core").reshape(1),
         back,

time: 355 us -> 355 us (level)
  no operation moved by 1% of the time
where the time goes in v4:
time: 355 us
  waiting for transfers between devices  275 us (77%)
  Pallas kernels  44.9 us (13%)
  starting transfers between devices  34.8 us (10%)
    all_to_all x1, waiting for transfers between devices, shards(): back = exchange(prod.reshape(hidden, rows, total))  95.2 us
    all_to_all x1, waiting for transfers between devices, shards(): exchange(left).reshape(matrix)  95.2 us
    all_to_all x1, waiting for transfers between devices, shards(): own = exchange(right)  84.4 us
    pallas_call x2, Pallas kernels, enter(): pl.pallas_call(enter_kernel, grid=(total // width,), in_specs=[pair_spec,...  21.8 us
    all_to_all x1, starting transfers between devices, shards(): own = exchange(right)  15.8 us
    pallas_call x1, Pallas kernels, product(): pl.pallas_call(functools.partial(product_kernel, steps), grid=(2 * steps,...  14 us
    all_to_all x1, starting transfers between devices, shards(): back = exchange(prod.reshape(hidden, rows, total))  9.58 us
    all_to_all x1, starting transfers between devices, shards(): exchange(left).reshape(matrix)  9.31 us
  transfers between devices with their start and end apart: 4, of which 3 were waited for; matrix products, arithmetic and copies ran while one was open for 0% of the time, Pallas kernels for 3%

profile of v4, /device:TPU:6, one launch (start us, length us, event | category | flops | bytes accessed | tf_op | source)
XLA Modules:
  0.0 354.7 jit_solution(9006309421160761774)
XLA Ops:
  0.0 10.7 %enter_right.1 = bf16[128,8,2048]{2,1,0:T(8,128)(2,1)} custom-call(bf16[8,2048,128]{2,1,0:T(8,128)(2,1)} %pair_ref.3, s32[8,2048]{1,0:T(8,128)} %mask_ref.3, f32[1,128]{1,0:T(1,128)} %bitcast.13, f32[1,128]{1,0:T(1,128)} %bitcast.15, bf16[128,512]{1,0:T(8,128)(2,1)} %w_ref.3), custom_call_target="tpu_custom_call" | custom-call | flops 1073741824 | bytes 12582912 | tf_op jit(solution)/shard_map/enter_right/pallas_call | solution.py:89
  10.7 15.8 %all-to-all-start.1 = ((bf16[128,8,2048]{2,1,0:T(8,128)(2,1)}), bf16[128,8,2048]{2,1,0:T(8,128)(2,1)}, u32[]{:S(2)}, u32[]{:S(2)}) async-start(bf16[128,8,2048]{2,1,0:T(8,128)(2,1)} %enter_right.1), calls=%async_computation.1 | async-start | bytes 8388608 | tf_op jit(solution)/shard_map/all_to_all | solution.py:212
  26.6 11.1 %enter_left.1 = (bf16[128,8,2048]{2,1,0:T(8,128)(2,1)}, bf16[8,2048,128]{2,1,0:T(8,128)(2,1)}) custom-call(bf16[8,2048,128]{2,1,0:T(8,128)(2,1)} %pair_ref.3, s32[8,2048]{1,0:T(8,128)} %mask_ref.3, f32[1,128]{1,0:T(1,128)} %bitcast.14, f32[1,128]{1,0:T(1,128)} %bitcast.16, bf16[128,512]{1,0:T(8,128)(2,1)} %w_ref.3), custom_call_target="tpu_custom_call" | custom-call | flops 1073741824 | bytes 12582912 | tf_op jit(solution)/shard_map/enter_left/pallas_call | solution.py:89
  37.6 84.4 %all-to-all-done.1 = bf16[128,8,2048]{2,1,0:T(8,128)(2,1)} async-done(((bf16[128,8,2048]{2,1,0:T(8,128)(2,1)}), bf16[128,8,2048]{2,1,0:T(8,128)(2,1)}, u32[]{:S(2)}, u32[]{:S(2)}) %all-to-all-start.1) | async-done | bytes 4194336 | tf_op jit(solution)/shard_map/all_to_all | solution.py:212
  122.1 9.3 %all-to-all-start = ((bf16[128,8,2048]{2,1,0:T(8,128)(2,1)}), bf16[128,8,2048]{2,1,0:T(8,128)(2,1)}, u32[]{:S(2)}, u32[]{:S(2)}) async-start(bf16[128,8,2048]{2,1,0:T(8,128)(2,1)} %get-tuple-element.31), calls=%async_computation | async-start | bytes 8388608 | tf_op jit(solution)/shard_map/all_to_all | solution.py:214
  131.4 0.1 collective-permute-start
  131.5 95.2 %all-to-all-done = bf16[128,8,2048]{2,1,0:T(8,128)(2,1)} async-done(((bf16[128,8,2048]{2,1,0:T(8,128)(2,1)}), bf16[128,8,2048]{2,1,0:T(8,128)(2,1)}, u32[]{:S(2)}, u32[]{:S(2)}) %all-to-all-start) | async-done | bytes 4194336 | tf_op jit(solution)/shard_map/all_to_all | solution.py:214
  226.7 0.0 collective-permute-done
  226.7 14.0 %product.1 = bf16[1024,2048]{1,0:T(8,128)(2,1)} custom-call(bf16[1024,2048]{1,0:T(8,128)(2,1)} %bitcast.3.a_ref, bf16[1024,2048]{1,0:T(8,128)(2,1)} %bitcast.4.own_ref, bf16[1024,2048]{1,0:T(8,128)(2,1)} %bitcast.5.other_ref), custom_call_target="tpu_custom_call" | custom-call | flops 8589934592 | bytes 16777216 | tf_op jit(solution)/shard_map/product/pallas_call | solution.py:129
  240.7 0.0 copy-start.1
  240.7 0.0 copy-start.2
  240.7 9.6 %all-to-all-start.2 = ((bf16[128,8,2048]{2,1,0:T(8,128)(2,1)}), bf16[128,8,2048]{2,1,0:T(8,128)(2,1)}, u32[]{:S(2)}, u32[]{:S(2)}) async-start(bf16[128,8,2048]{2,1,0:T(8,128)(2,1)} %bitcast.12), calls=%async_computation.2 | async-start | bytes 8388608 | tf_op jit(solution)/shard_map/all_to_all | solution.py:215
  250.3 0.0 copy-done.1
  250.4 0.0 copy-done.2
  250.4 0.0 copy-start
  250.4 95.2 %all-to-all-done.2.prod_ref = bf16[128,8,2048]{2,1,0:T(8,128)(2,1)} async-done(((bf16[128,8,2048]{2,1,0:T(8,128)(2,1)}), bf16[128,8,2048]{2,1,0:T(8,128)(2,1)}, u32[]{:S(2)}, u32[]{:S(2)}) %all-to-all-start.2) | async-done | bytes 4194336 | tf_op jit(solution)/shard_map/all_to_all | solution.py:215
  345.6 0.0 copy-done
  345.6 9.0 %leave.1 = bf16[8,32,2,32,128]{4,3,2,1,0:T(8,128)(2,1)} custom-call(s32[1]{0:T(128)} %bitcast.core_ref, bf16[128,8,2048]{2,1,0:T(8,128)(2,1)} %all-to-all-done.2.prod_ref, bf16[8,32,2,32,128]{4,3,2,1,0:T(8,128)(2,1)} %bitcast.11, f32[1,128]{1,0:T(1,128)} %bitcast.17, f32[1,128]{1,0:T(1,128)} %bitcast.18, bf16[256,256]{1,0:T(8,128)(2,1)} %copy-done), custom_call_target="tpu_custom_call" | custom-call | flops 1073741824 | bytes 12582912 | tf_op jit(solution)/shard_map/leave/pallas_call | solution.py:182
  (3 shorter events, 0.0 us)
Async XLA Ops:
  10.7 111.4 %all-to-all-start.1 = ((bf16[128,8,2048]{2,1,0:T(8,128)(2,1)}), bf16[128,8,2048]{2,1,0:T(8,128)(2,1)}, u32[]{:S(2)}, u32[]{:S(2)}) async-start(bf16[128,8,2048]{2,1,0:T(8,128)(2,1)} %enter_right.1), calls=%async_computation.1 | async-start | bytes 8388608 | tf_op jit(solution)/shard_map/all_to_all | solution.py:212
  122.1 104.6 %all-to-all-start = ((bf16[128,8,2048]{2,1,0:T(8,128)(2,1)}), bf16[128,8,2048]{2,1,0:T(8,128)(2,1)}, u32[]{:S(2)}, u32[]{:S(2)}) async-start(bf16[128,8,2048]{2,1,0:T(8,128)(2,1)} %get-tuple-element.31), calls=%async_computation | async-start | bytes 8388608 | tf_op jit(solution)/shard_map/all_to_all | solution.py:214
  131.4 95.3 %collective-permute-start = (bf16[128,8,2048]{2,1,0:T(8,128)(2,1)}, bf16[128,8,2048]{2,1,0:T(8,128)(2,1)}, u32[]{:S(2)}, u32[]{:S(2)}) collective-permute-start(bf16[128,8,2048]{2,1,0:T(8,128)(2,1)} %all-to-all-done.1), channel_id=1, source_target_pairs={{0,4},{4,0},{1,5},{5,1},{2,6},{6,2},{3,7},{7,3},{8,12},{12,8},{9,1... | collective-permute-start | bytes 12582920 | tf_op jit(solution)/shard_map/ppermute | solution.py:213
  240.7 9.6 %copy-start.1 = (bf16[128,128]{1,0:T(8,128)(2,1)S(1)}, bf16[128,128]{1,0:T(8,128)(2,1)}, u32[]{:S(2)}) copy-start(bf16[128,128]{1,0:T(8,128)(2,1)} %param.21) | copy-start | bytes 98308
  240.7 9.6 %copy-start.2 = (bf16[128,128]{1,0:T(8,128)(2,1)S(1)}, bf16[128,128]{1,0:T(8,128)(2,1)}, u32[]{:S(2)}) copy-start(bf16[128,128]{1,0:T(8,128)(2,1)} %param.18) | copy-start | bytes 98308
  240.7 104.9 %all-to-all-start.2 = ((bf16[128,8,2048]{2,1,0:T(8,128)(2,1)}), bf16[128,8,2048]{2,1,0:T(8,128)(2,1)}, u32[]{:S(2)}, u32[]{:S(2)}) async-start(bf16[128,8,2048]{2,1,0:T(8,128)(2,1)} %bitcast.12), calls=%async_computation.2 | async-start | bytes 8388608 | tf_op jit(solution)/shard_map/all_to_all | solution.py:215
  250.4 95.2 %copy-start = (bf16[256,256]{1,0:T(8,128)(2,1)}, bf16[256,256]{1,0:T(8,128)(2,1)S(1)}, u32[]{:S(2)}) copy-start(bf16[256,256]{1,0:T(8,128)(2,1)S(1)} %multiply_dynamic-update-slice_fusion.w_ref) | copy-start | bytes 393220

commit v5 on v4

--- a/solution.py
+++ b/solution.py
@@ -16,9 +16,11 @@
 VMEM_LIMIT = 56 * MIB
 
 
-def rows_norm(x, gain, bias):
-    average = jnp.mean(x, axis=-1, keepdims=True)
-    centred = x - average
+def rows_norm(values, gain, bias):
+    channels = values.shape[-1]
+    share = jnp.full((channels, channels), 1.0 / channels, jnp.bfloat16)
+    average = jnp.dot(values, share, preferred_element_type=jnp.float32)
+    centred = values.astype(jnp.float32) - average
     spread = jnp.mean(centred * centred, axis=-1, keepdims=True)
     return centred * lax.rsqrt(spread + 1e-05) * gain + bias
 
@@ -61,7 +63,7 @@
     weights = turned(w_ref, w_scr)
     keep = mask_ref[...].astype(jnp.float32)
     rows, width, channels = pair_ref.shape
-    values = pair_ref[...].reshape(rows * width, channels).astype(jnp.float32)
+    values = pair_ref[...].reshape(rows * width, channels)
     normed = rows_norm(values, gain_ref[...], bias_ref[...]).astype(jnp.bfloat16)
     for i in range(rows):
         part = normed[i * width : (i + 1) * width]

time: 355 us -> 354 us (level)
  no operation moved by 1% of the time
where the time goes in v5:
time: 354 us; the launch traced here: 353 us
  waiting for transfers between devices  276 us (78%)
  Pallas kernels  42.4 us (12%)
  starting transfers between devices  34.8 us (10%)
    all_to_all x1, waiting for transfers between devices, shards(): back = exchange(prod.reshape(hidden, rows, total))  95.2 us
    all_to_all x1, waiting for transfers between devices, shards(): exchange(left).reshape(matrix)  95.2 us
    all_to_all x1, waiting for transfers between devices, shards(): own = exchange(right)  85.5 us
    pallas_call x2, Pallas kernels, enter(): pl.pallas_call(enter_kernel, grid=(total // width,), in_specs=[pair_spec,...  19.3 us
    all_to_all x1, starting transfers between devices, shards(): own = exchange(right)  15.8 us
    pallas_call x1, Pallas kernels, product(): pl.pallas_call(functools.partial(product_kernel, steps), grid=(2 * steps,...  14 us
    all_to_all x1, starting transfers between devices, shards(): back = exchange(prod.reshape(hidden, rows, total))  9.58 us
    all_to_all x1, starting transfers between devices, shards(): exchange(left).reshape(matrix)  9.31 us
  transfers between devices with their start and end apart: 4, of which 3 were waited for; matrix products, arithmetic and copies ran while one was open for 0% of the time, Pallas kernels for 3%

profile of v5, /device:TPU:6, one launch (start us, length us, event | category | flops | bytes accessed | tf_op | source)
XLA Modules:
  0.0 353.3 jit_solution(9199931041366642359)
XLA Ops:
  0.0 9.3 %enter_right.1 = bf16[128,8,2048]{2,1,0:T(8,128)(2,1)} custom-call(bf16[8,2048,128]{2,1,0:T(8,128)(2,1)} %pair_ref.3, s32[8,2048]{1,0:T(8,128)} %mask_ref.3, f32[1,128]{1,0:T(1,128)} %bitcast.13, f32[1,128]{1,0:T(1,128)} %bitcast.15, bf16[128,512]{1,0:T(8,128)(2,1)} %w_ref.3), custom_call_target="tpu_custom_call" | custom-call | flops 1073741824 | bytes 12582912 | tf_op jit(solution)/shard_map/enter_right/pallas_call | solution.py:91
  9.3 15.8 %all-to-all-start.1 = ((bf16[128,8,2048]{2,1,0:T(8,128)(2,1)}), bf16[128,8,2048]{2,1,0:T(8,128)(2,1)}, u32[]{:S(2)}, u32[]{:S(2)}) async-start(bf16[128,8,2048]{2,1,0:T(8,128)(2,1)} %enter_right.1), calls=%async_computation.1 | async-start | bytes 8388608 | tf_op jit(solution)/shard_map/all_to_all | solution.py:214
  25.1 10.0 %enter_left.1 = (bf16[128,8,2048]{2,1,0:T(8,128)(2,1)}, bf16[8,2048,128]{2,1,0:T(8,128)(2,1)}) custom-call(bf16[8,2048,128]{2,1,0:T(8,128)(2,1)} %pair_ref.3, s32[8,2048]{1,0:T(8,128)} %mask_ref.3, f32[1,128]{1,0:T(1,128)} %bitcast.14, f32[1,128]{1,0:T(1,128)} %bitcast.16, bf16[128,512]{1,0:T(8,128)(2,1)} %w_ref.3), custom_call_target="tpu_custom_call" | custom-call | flops 1073741824 | bytes 12582912 | tf_op jit(solution)/shard_map/enter_left/pallas_call | solution.py:91
  35.1 85.5 %all-to-all-done.1 = bf16[128,8,2048]{2,1,0:T(8,128)(2,1)} async-done(((bf16[128,8,2048]{2,1,0:T(8,128)(2,1)}), bf16[128,8,2048]{2,1,0:T(8,128)(2,1)}, u32[]{:S(2)}, u32[]{:S(2)}) %all-to-all-start.1) | async-done | bytes 4194336 | tf_op jit(solution)/shard_map/all_to_all | solution.py:214
  120.7 9.3 %all-to-all-start = ((bf16[128,8,2048]{2,1,0:T(8,128)(2,1)}), bf16[128,8,2048]{2,1,0:T(8,128)(2,1)}, u32[]{:S(2)}, u32[]{:S(2)}) async-start(bf16[128,8,2048]{2,1,0:T(8,128)(2,1)} %get-tuple-element.31), calls=%async_computation | async-start | bytes 8388608 | tf_op jit(solution)/shard_map/all_to_all | solution.py:216
  130.0 0.1 collective-permute-start
  130.1 95.2 %all-to-all-done = bf16[128,8,2048]{2,1,0:T(8,128)(2,1)} async-done(((bf16[128,8,2048]{2,1,0:T(8,128)(2,1)}), bf16[128,8,2048]{2,1,0:T(8,128)(2,1)}, u32[]{:S(2)}, u32[]{:S(2)}) %all-to-all-start) | async-done | bytes 4194336 | tf_op jit(solution)/shard_map/all_to_all | solution.py:216
  225.3 0.0 collective-permute-done
  225.3 14.0 %product.1 = bf16[1024,2048]{1,0:T(8,128)(2,1)} custom-call(bf16[1024,2048]{1,0:T(8,128)(2,1)} %bitcast.3.a_ref, bf16[1024,2048]{1,0:T(8,128)(2,1)} %bitcast.4.own_ref, bf16[1024,2048]{1,0:T(8,128)(2,1)} %bitcast.5.other_ref), custom_call_target="tpu_custom_call" | custom-call | flops 8589934592 | bytes 16777216 | tf_op jit(solution)/shard_map/product/pallas_call | solution.py:131
  239.3 0.0 copy-start.1
  239.3 0.0 copy-start.2
  239.3 9.6 %all-to-all-start.2 = ((bf16[128,8,2048]{2,1,0:T(8,128)(2,1)}), bf16[128,8,2048]{2,1,0:T(8,128)(2,1)}, u32[]{:S(2)}, u32[]{:S(2)}) async-start(bf16[128,8,2048]{2,1,0:T(8,128)(2,1)} %bitcast.12), calls=%async_computation.2 | async-start | bytes 8388608 | tf_op jit(solution)/shard_map/all_to_all | solution.py:217
  248.9 0.0 copy-done.1
  248.9 0.0 copy-done.2
  249.0 0.0 copy-start
  249.0 95.2 %all-to-all-done.2.prod_ref = bf16[128,8,2048]{2,1,0:T(8,128)(2,1)} async-done(((bf16[128,8,2048]{2,1,0:T(8,128)(2,1)}), bf16[128,8,2048]{2,1,0:T(8,128)(2,1)}, u32[]{:S(2)}, u32[]{:S(2)}) %all-to-all-start.2) | async-done | bytes 4194336 | tf_op jit(solution)/shard_map/all_to_all | solution.py:217
  344.2 0.0 copy-done
  344.2 9.0 %leave.1 = bf16[8,32,2,32,128]{4,3,2,1,0:T(8,128)(2,1)} custom-call(s32[1]{0:T(128)} %bitcast.core_ref, bf16[128,8,2048]{2,1,0:T(8,128)(2,1)} %all-to-all-done.2.prod_ref, bf16[8,32,2,32,128]{4,3,2,1,0:T(8,128)(2,1)} %bitcast.11, f32[1,128]{1,0:T(1,128)} %bitcast.17, f32[1,128]{1,0:T(1,128)} %bitcast.18, bf16[256,256]{1,0:T(8,128)(2,1)} %copy-done), custom_call_target="tpu_custom_call" | custom-call | flops 1073741824 | bytes 12582912 | tf_op jit(solution)/shard_map/leave/pallas_call | solution.py:184
  (3 shorter events, 0.0 us)
Async XLA Ops:
  9.3 111.4 %all-to-all-start.1 = ((bf16[128,8,2048]{2,1,0:T(8,128)(2,1)}), bf16[128,8,2048]{2,1,0:T(8,128)(2,1)}, u32[]{:S(2)}, u32[]{:S(2)}) async-start(bf16[128,8,2048]{2,1,0:T(8,128)(2,1)} %enter_right.1), calls=%async_computation.1 | async-start | bytes 8388608 | tf_op jit(solution)/shard_map/all_to_all | solution.py:214
  120.7 104.6 %all-to-all-start = ((bf16[128,8,2048]{2,1,0:T(8,128)(2,1)}), bf16[128,8,2048]{2,1,0:T(8,128)(2,1)}, u32[]{:S(2)}, u32[]{:S(2)}) async-start(bf16[128,8,2048]{2,1,0:T(8,128)(2,1)} %get-tuple-element.31), calls=%async_computation | async-start | bytes 8388608 | tf_op jit(solution)/shard_map/all_to_all | solution.py:216
  130.0 95.3 %collective-permute-start = (bf16[128,8,2048]{2,1,0:T(8,128)(2,1)}, bf16[128,8,2048]{2,1,0:T(8,128)(2,1)}, u32[]{:S(2)}, u32[]{:S(2)}) collective-permute-start(bf16[128,8,2048]{2,1,0:T(8,128)(2,1)} %all-to-all-done.1), channel_id=1, source_target_pairs={{0,4},{4,0},{1,5},{5,1},{2,6},{6,2},{3,7},{7,3},{8,12},{12,8},{9,1... | collective-permute-start | bytes 12582920 | tf_op jit(solution)/shard_map/ppermute | solution.py:215
  239.3 9.6 %copy-start.1 = (bf16[128,128]{1,0:T(8,128)(2,1)S(1)}, bf16[128,128]{1,0:T(8,128)(2,1)}, u32[]{:S(2)}) copy-start(bf16[128,128]{1,0:T(8,128)(2,1)} %param.21) | copy-start | bytes 98308
  239.3 9.6 %copy-start.2 = (bf16[128,128]{1,0:T(8,128)(2,1)S(1)}, bf16[128,128]{1,0:T(8,128)(2,1)}, u32[]{:S(2)}) copy-start(bf16[128,128]{1,0:T(8,128)(2,1)} %param.18) | copy-start | bytes 98308
  239.3 104.9 %all-to-all-start.2 = ((bf16[128,8,2048]{2,1,0:T(8,128)(2,1)}), bf16[128,8,2048]{2,1,0:T(8,128)(2,1)}, u32[]{:S(2)}, u32[]{:S(2)}) async-start(bf16[128,8,2048]{2,1,0:T(8,128)(2,1)} %bitcast.12), calls=%async_computation.2 | async-start | bytes 8388608 | tf_op jit(solution)/shard_map/all_to_all | solution.py:217
  249.0 95.2 %copy-start = (bf16[256,256]{1,0:T(8,128)(2,1)}, bf16[256,256]{1,0:T(8,128)(2,1)S(1)}, u32[]{:S(2)}) copy-start(bf16[256,256]{1,0:T(8,128)(2,1)S(1)} %multiply_dynamic-update-slice_fusion.w_ref) | copy-start | bytes 393220

commit v6 on v5

--- a/solution.py
+++ b/solution.py
@@ -26,7 +26,7 @@
 
 
 def gate_by(half_gate, half_value):
-    return (jnp.tanh(half_gate) + 1.0) * half_value
+    return half_value * jnp.tanh(half_gate) + half_value
 
 
 def turned(w_ref, turned_ref):

time: 354 us -> 354 us (level)
  no operation moved by 1% of the time
where the time goes in v6:
time: 354 us; the launch traced here: 353 us
  waiting for transfers between devices  276 us (78%)
  Pallas kernels  42.2 us (12%)
  starting transfers between devices  34.8 us (10%)
    all_to_all x1, waiting for transfers between devices, shards(): back = exchange(prod.reshape(hidden, rows, total))  95.2 us
    all_to_all x1, waiting for transfers between devices, shards(): exchange(left).reshape(matrix)  95.2 us
    all_to_all x1, waiting for transfers between devices, shards(): own = exchange(right)  85.6 us
    pallas_call x2, Pallas kernels, enter(): pl.pallas_call(enter_kernel, grid=(total // width,), in_specs=[pair_spec,...  19.2 us
    all_to_all x1, starting transfers between devices, shards(): own = exchange(right)  15.8 us
    pallas_call x1, Pallas kernels, product(): pl.pallas_call(functools.partial(product_kernel, steps), grid=(2 * steps,...  14 us
    all_to_all x1, starting transfers between devices, shards(): back = exchange(prod.reshape(hidden, rows, total))  9.58 us
    all_to_all x1, starting transfers between devices, shards(): exchange(left).reshape(matrix)  9.31 us
  transfers between devices with their start and end apart: 4, of which 3 were waited for; matrix products, arithmetic and copies ran while one was open for 0% of the time, Pallas kernels for 3%

profile of v6, /device:TPU:6, one launch (start us, length us, event | category | flops | bytes accessed | tf_op | source)
XLA Modules:
  0.0 353.2 jit_solution(11900285122478766626)
XLA Ops:
  0.0 9.2 %enter_right.1 = bf16[128,8,2048]{2,1,0:T(8,128)(2,1)} custom-call(bf16[8,2048,128]{2,1,0:T(8,128)(2,1)} %pair_ref.3, s32[8,2048]{1,0:T(8,128)} %mask_ref.3, f32[1,128]{1,0:T(1,128)} %bitcast.13, f32[1,128]{1,0:T(1,128)} %bitcast.15, bf16[128,512]{1,0:T(8,128)(2,1)} %w_ref.3), custom_call_target="tpu_custom_call" | custom-call | flops 1073741824 | bytes 12582912 | tf_op jit(solution)/shard_map/enter_right/pallas_call | solution.py:91
  9.2 15.8 %all-to-all-start.1 = ((bf16[128,8,2048]{2,1,0:T(8,128)(2,1)}), bf16[128,8,2048]{2,1,0:T(8,128)(2,1)}, u32[]{:S(2)}, u32[]{:S(2)}) async-start(bf16[128,8,2048]{2,1,0:T(8,128)(2,1)} %enter_right.1), calls=%async_computation.1 | async-start | bytes 8388608 | tf_op jit(solution)/shard_map/all_to_all | solution.py:214
  25.1 9.9 %enter_left.1 = (bf16[128,8,2048]{2,1,0:T(8,128)(2,1)}, bf16[8,2048,128]{2,1,0:T(8,128)(2,1)}) custom-call(bf16[8,2048,128]{2,1,0:T(8,128)(2,1)} %pair_ref.3, s32[8,2048]{1,0:T(8,128)} %mask_ref.3, f32[1,128]{1,0:T(1,128)} %bitcast.14, f32[1,128]{1,0:T(1,128)} %bitcast.16, bf16[128,512]{1,0:T(8,128)(2,1)} %w_ref.3), custom_call_target="tpu_custom_call" | custom-call | flops 1073741824 | bytes 12582912 | tf_op jit(solution)/shard_map/enter_left/pallas_call | solution.py:91
  35.0 85.6 %all-to-all-done.1 = bf16[128,8,2048]{2,1,0:T(8,128)(2,1)} async-done(((bf16[128,8,2048]{2,1,0:T(8,128)(2,1)}), bf16[128,8,2048]{2,1,0:T(8,128)(2,1)}, u32[]{:S(2)}, u32[]{:S(2)}) %all-to-all-start.1) | async-done | bytes 4194336 | tf_op jit(solution)/shard_map/all_to_all | solution.py:214
  120.6 9.3 %all-to-all-start = ((bf16[128,8,2048]{2,1,0:T(8,128)(2,1)}), bf16[128,8,2048]{2,1,0:T(8,128)(2,1)}, u32[]{:S(2)}, u32[]{:S(2)}) async-start(bf16[128,8,2048]{2,1,0:T(8,128)(2,1)} %get-tuple-element.31), calls=%async_computation | async-start | bytes 8388608 | tf_op jit(solution)/shard_map/all_to_all | solution.py:216
  129.9 0.1 collective-permute-start
  130.0 95.2 %all-to-all-done = bf16[128,8,2048]{2,1,0:T(8,128)(2,1)} async-done(((bf16[128,8,2048]{2,1,0:T(8,128)(2,1)}), bf16[128,8,2048]{2,1,0:T(8,128)(2,1)}, u32[]{:S(2)}, u32[]{:S(2)}) %all-to-all-start) | async-done | bytes 4194336 | tf_op jit(solution)/shard_map/all_to_all | solution.py:216
  225.2 0.0 collective-permute-done
  225.2 14.0 %product.1 = bf16[1024,2048]{1,0:T(8,128)(2,1)} custom-call(bf16[1024,2048]{1,0:T(8,128)(2,1)} %bitcast.3.a_ref, bf16[1024,2048]{1,0:T(8,128)(2,1)} %bitcast.4.own_ref, bf16[1024,2048]{1,0:T(8,128)(2,1)} %bitcast.5.other_ref), custom_call_target="tpu_custom_call" | custom-call | flops 8589934592 | bytes 16777216 | tf_op jit(solution)/shard_map/product/pallas_call | solution.py:131
  239.2 0.0 copy-start.1
  239.2 0.0 copy-start.2
  239.2 9.6 %all-to-all-start.2 = ((bf16[128,8,2048]{2,1,0:T(8,128)(2,1)}), bf16[128,8,2048]{2,1,0:T(8,128)(2,1)}, u32[]{:S(2)}, u32[]{:S(2)}) async-start(bf16[128,8,2048]{2,1,0:T(8,128)(2,1)} %bitcast.12), calls=%async_computation.2 | async-start | bytes 8388608 | tf_op jit(solution)/shard_map/all_to_all | solution.py:217
  248.8 0.0 copy-done.1
  248.9 0.0 copy-done.2
  248.9 0.0 copy-start
  248.9 95.2 %all-to-all-done.2.prod_ref = bf16[128,8,2048]{2,1,0:T(8,128)(2,1)} async-done(((bf16[128,8,2048]{2,1,0:T(8,128)(2,1)}), bf16[128,8,2048]{2,1,0:T(8,128)(2,1)}, u32[]{:S(2)}, u32[]{:S(2)}) %all-to-all-start.2) | async-done | bytes 4194336 | tf_op jit(solution)/shard_map/all_to_all | solution.py:217
  344.1 0.0 copy-done
  344.1 9.0 %leave.1 = bf16[8,32,2,32,128]{4,3,2,1,0:T(8,128)(2,1)} custom-call(s32[1]{0:T(128)} %bitcast.core_ref, bf16[128,8,2048]{2,1,0:T(8,128)(2,1)} %all-to-all-done.2.prod_ref, bf16[8,32,2,32,128]{4,3,2,1,0:T(8,128)(2,1)} %bitcast.11, f32[1,128]{1,0:T(1,128)} %bitcast.17, f32[1,128]{1,0:T(1,128)} %bitcast.18, bf16[256,256]{1,0:T(8,128)(2,1)} %copy-done), custom_call_target="tpu_custom_call" | custom-call | flops 1073741824 | bytes 12582912 | tf_op jit(solution)/shard_map/leave/pallas_call | solution.py:184
  (3 shorter events, 0.0 us)
Async XLA Ops:
  9.2 111.4 %all-to-all-start.1 = ((bf16[128,8,2048]{2,1,0:T(8,128)(2,1)}), bf16[128,8,2048]{2,1,0:T(8,128)(2,1)}, u32[]{:S(2)}, u32[]{:S(2)}) async-start(bf16[128,8,2048]{2,1,0:T(8,128)(2,1)} %enter_right.1), calls=%async_computation.1 | async-start | bytes 8388608 | tf_op jit(solution)/shard_map/all_to_all | solution.py:214
  120.6 104.6 %all-to-all-start = ((bf16[128,8,2048]{2,1,0:T(8,128)(2,1)}), bf16[128,8,2048]{2,1,0:T(8,128)(2,1)}, u32[]{:S(2)}, u32[]{:S(2)}) async-start(bf16[128,8,2048]{2,1,0:T(8,128)(2,1)} %get-tuple-element.31), calls=%async_computation | async-start | bytes 8388608 | tf_op jit(solution)/shard_map/all_to_all | solution.py:216
  129.9 95.3 %collective-permute-start = (bf16[128,8,2048]{2,1,0:T(8,128)(2,1)}, bf16[128,8,2048]{2,1,0:T(8,128)(2,1)}, u32[]{:S(2)}, u32[]{:S(2)}) collective-permute-start(bf16[128,8,2048]{2,1,0:T(8,128)(2,1)} %all-to-all-done.1), channel_id=1, source_target_pairs={{0,4},{4,0},{1,5},{5,1},{2,6},{6,2},{3,7},{7,3},{8,12},{12,8},{9,1... | collective-permute-start | bytes 12582920 | tf_op jit(solution)/shard_map/ppermute | solution.py:215
  239.2 9.6 %copy-start.1 = (bf16[128,128]{1,0:T(8,128)(2,1)S(1)}, bf16[128,128]{1,0:T(8,128)(2,1)}, u32[]{:S(2)}) copy-start(bf16[128,128]{1,0:T(8,128)(2,1)} %param.21) | copy-start | bytes 98308
  239.2 9.6 %copy-start.2 = (bf16[128,128]{1,0:T(8,128)(2,1)S(1)}, bf16[128,128]{1,0:T(8,128)(2,1)}, u32[]{:S(2)}) copy-start(bf16[128,128]{1,0:T(8,128)(2,1)} %param.18) | copy-start | bytes 98308
  239.2 104.9 %all-to-all-start.2 = ((bf16[128,8,2048]{2,1,0:T(8,128)(2,1)}), bf16[128,8,2048]{2,1,0:T(8,128)(2,1)}, u32[]{:S(2)}, u32[]{:S(2)}) async-start(bf16[128,8,2048]{2,1,0:T(8,128)(2,1)} %bitcast.12), calls=%async_computation.2 | async-start | bytes 8388608 | tf_op jit(solution)/shard_map/all_to_all | solution.py:217
  248.9 95.2 %copy-start = (bf16[256,256]{1,0:T(8,128)(2,1)}, bf16[256,256]{1,0:T(8,128)(2,1)S(1)}, u32[]{:S(2)}) copy-start(bf16[256,256]{1,0:T(8,128)(2,1)S(1)} %multiply_dynamic-update-slice_fusion.w_ref) | copy-start | bytes 393220
